TPU v7x, 32 devices: a whole 2x2x4 slice. The times are simulated.
32 devices in a mesh: dom: 16 (over z, y, x), feat: 2 (over core).
Axes of the slice: x: 2, y: 2, z: 4, core: 2. Of those that a mesh axis runs over, the one named last changes fastest.
Arguments:
- features: bfloat16 [2048, 128], P('dom'), may hold values from -6 to 6
- w_self: bfloat16 [128, 256], P(None, 'feat'), may hold values from -0.5 to 0.5
- w_neigh: bfloat16 [128, 256], P(None, 'feat'), may hold values from -6 to 6
- tiles: bfloat16 [256, 128, 128], P('dom'), may hold values from 0 to 1, as said below
- dest: int32 [256, 1], P('dom'), may hold values from 0 to 15; in each aligned block of 16 rows (0 to 15, 16 to 31, ...) at most 2 rows name the same one
- outside: int32 [2048], P('dom'), may hold values from 1 to 256
- cotangent: bfloat16 [2048, 256], P('dom', 'feat'), may hold values from -6 to 6
Outputs:
- output: bfloat16 [2048, 256], P('dom', 'feat')
- grad_input: bfloat16 [2048, 128], P('dom')
- grad_self: float32 [128, 256], P(None, 'feat')
- grad_neigh: float32 [128, 256], P(None, 'feat')
Inputs may be any that keep to these rules, and one draw needn't show every extreme that they name: `dest`: among the 16 tiles of one index of dom, at most 2 name one destination block, and some block is named by exactly 2. `tiles`: entries are 0 or 1.
All inputs are finite; a program needn't handle non-finite values.
Results may differ from a plain program's by a relative error of at most 0.015.
Values may be sent and summed in bfloat16 or wider, within the bound.
No kernel may reach another device: no remote copies, remote signals or barrier semaphores. Data moves between devices by JAX's collectives and lax.ppermute only.
A program may use at most 128 MiB of HBM per device.

v0:
```python
import jax
import jax.numpy as jnp
from jax import lax
from jax.sharding import PartitionSpec as P

CAP = 2


def on_device(features, w_self, w_neigh, tiles, dest, outside, cotangent):
    peers = lax.axis_size("dom")
    tile_count, rows, _ = tiles.shape
    hidden_local = w_self.shape[1]
    self_part = jnp.dot(features, w_self, preferred_element_type=jnp.float32)
    message = jnp.dot(features, w_neigh, preferred_element_type=jnp.float32).astype(jnp.bfloat16)
    targets = dest[:, 0]
    dest_onehot = (targets[:, None] == jnp.arange(peers, dtype=jnp.int32)[None, :]).astype(
        jnp.bfloat16
    )
    flat_tiles = tiles.reshape(tile_count, rows * rows)
    dest_tiles = jnp.einsum(
        "td,tij->idj", dest_onehot, tiles, preferred_element_type=jnp.float32
    ).astype(jnp.bfloat16)
    counts = dest_onehot.astype(jnp.int32)
    before = jnp.cumsum(counts, axis=0) - counts
    rank = jnp.sum(before * counts, axis=1)
    slot = targets * CAP + rank
    slot_onehot = (slot[None, :] == jnp.arange(peers * CAP, dtype=jnp.int32)[:, None]).astype(
        jnp.bfloat16
    )
    slot_tiles = jnp.dot(slot_onehot, flat_tiles, preferred_element_type=jnp.float32).astype(
        jnp.bfloat16
    )
    slot_tiles = slot_tiles.reshape(peers * CAP, rows, rows)
    slot_links = jnp.sum(slot_tiles.astype(jnp.float32), axis=1).reshape(peers, CAP * rows)
    partial_sums = jnp.einsum(
        "sij,ik->sjk", slot_tiles, message, preferred_element_type=jnp.float32
    )
    partial_sums = partial_sums.reshape(peers, CAP * rows, hidden_local)
    arrived, arrived_links = (
        lax.all_to_all(partial_sums, "dom", split_axis=0, concat_axis=0, tiled=True),
        lax.all_to_all(slot_links, "dom", split_axis=0, concat_axis=0, tiled=True),
    )
    summed = jnp.sum(arrived.reshape(peers * CAP, rows, hidden_local), axis=0)
    links = jnp.sum(arrived_links.reshape(peers * CAP, rows), axis=0)
    inverse = 1.0 / (links + outside.astype(jnp.float32))
    pre = self_part + summed * inverse[:, None]
    sigma = jax.nn.sigmoid(pre)
    output = (pre * sigma).astype(jnp.bfloat16)
    dpre = (cotangent.astype(jnp.float32) * sigma * (1.0 + pre * (1.0 - sigma))).astype(
        jnp.bfloat16
    )
    dagg = (dpre.astype(jnp.float32) * inverse[:, None]).astype(jnp.bfloat16)
    dest_columns = dest_tiles.reshape(rows, peers * rows)
    dmessage = jnp.dot(
        dest_columns,
        lax.all_gather(dagg, "dom", axis=0, tiled=True),
        preferred_element_type=jnp.float32,
    )
    dmessage = dmessage.astype(jnp.bfloat16)
    both_grads = jnp.concatenate([dpre, dmessage], axis=1)
    local_term = lax.dot_general(
        features, both_grads, (((0,), (0,)), ((), ())), preferred_element_type=jnp.float32
    )
    weight_sum = lax.psum(local_term, "dom")
    grad_self = weight_sum[:, :hidden_local]
    grad_neigh = weight_sum[:, hidden_local:]
    input_term = lax.dot_general(
        dpre, w_self, (((1,), (1,)), ((), ())), preferred_element_type=jnp.float32
    )
    input_term = input_term + lax.dot_general(
        dmessage, w_neigh, (((1,), (1,)), ((), ())), preferred_element_type=jnp.float32
    )
    grad_input = lax.psum(input_term, "feat").astype(jnp.bfloat16)
    return (output, grad_input, grad_self, grad_neigh)


def solution(mesh):
    placed = (
        P("dom", None),
        P(None, "feat"),
        P(None, "feat"),
        P("dom", None, None),
        P("dom", None),
        P("dom"),
        P("dom", "feat"),
    )
    return jax.shard_map(
        on_device,
        mesh=mesh,
        in_specs=placed,
        out_specs=(P("dom", "feat"), P("dom", None), P(None, "feat"), P(None, "feat")),
        check_vma=False,
    )
```

profile of v0, /device:TPU:0, one launch (start us, length us, event | category | flops | bytes accessed | tf_op | source)
XLA Modules:
  0.0 231.8 jit_solution(8402888257171509871)
XLA Ops:
  7.2 0.0 copy-start
  7.2 0.7 fusion.16
  8.0 0.8 fusion.11
  8.8 0.7 multiply_add_fusion
  9.5 1.5 fusion
  11.0 0.2 copy.29
  11.2 0.0 copy-start.2
  11.2 0.9 convert_reduce_fusion
  12.1 8.3 %all-to-all-start.1 = ((f32[16,1,256]{2,1,0:T(1,128)}), f32[16,1,256]{2,1,0:T(1,128)S(1)}, u32[]{:S(2)}, u32[]{:S(2)}) async-start(f32[16,1,256]{2,1,0:T(1,128)} %bitcast.5), calls=%async_computation.1 | async-start | bytes 32768 | tf_op jit(solution)/shard_map/all_to_all | solution.py:41
  20.4 0.7 copy.18
  21.1 1.9 fusion.2
  23.0 4.7 %all-to-all-done.1 = f32[16,1,256]{2,1,0:T(1,128)S(1)} async-done(((f32[16,1,256]{2,1,0:T(1,128)}), f32[16,1,256]{2,1,0:T(1,128)S(1)}, u32[]{:S(2)}, u32[]{:S(2)}) %all-to-all-start.1) | async-done | bytes 16416 | tf_op jit(solution)/shard_map/all_to_all | solution.py:41
  27.7 3.7 %all-to-all-start = ((f32[16,256,128]{2,1,0:T(8,128)}), f32[16,256,128]{2,1,0:T(8,128)S(1)}, u32[]{:S(2)}, u32[]{:S(2)}) async-start(f32[16,256,128]{2,1,0:T(8,128)} %fusion.2), calls=%async_computation | async-start | bytes 4194304 | tf_op jit(solution)/shard_map/all_to_all | solution.py:40
  31.5 0.0 all-reduce.2.cloned.1.call-start
  31.5 0.1 copy.20
  31.7 0.5 convolution_convert_fusion.1
  32.2 41.5 %all-to-all-done = f32[16,256,128]{2,1,0:T(8,128)S(1)} async-done(((f32[16,256,128]{2,1,0:T(8,128)}), f32[16,256,128]{2,1,0:T(8,128)S(1)}, u32[]{:S(2)}, u32[]{:S(2)}) %all-to-all-start) | async-done | bytes 2097184 | tf_op jit(solution)/shard_map/all_to_all | solution.py:40
  73.7 0.1 reduce_sum.37
  73.8 0.1 copy.19
  73.9 0.2 multiply_convert_fusion
  74.2 0.2 fusion.20
  74.3 46.9 %all_gather.3 = bf16[2048,128]{0,1:T(8,128)(2,1)S(1)} all-gather(bf16[128,128]{0,1:T(8,128)(2,1)S(1)} %get-tuple-element.12), channel_id=1, replica_groups=mesh['dom'=16,'feat'=2] {'dom'}, dimensions={0}, use_global_device_ids=true | all-gather | bytes 557056 | tf_op jit(solution)/shard_map/all_gather | solution.py:56
  121.2 0.3 convolution_convert_fusion.2
  121.5 0.8 convolution_bitcast_fusion
  122.3 0.0 all-reduce.2.cloned.1.call-update
  122.3 0.2 convolution_add_fusion
  122.5 0.7 copy.23
  123.2 4.2 %psum.14 = bf16[128,128]{1,0:T(8,128)(2,1)} all-reduce(f32[128,128]{1,0:T(8,128)S(1)} %convolution_add_fusion), channel_id=1, replica_groups=mesh['dom'=16,'feat'=2] {'feat'}, use_global_device_ids=true, to_apply=%region_5.6 | all-reduce | flops 16384 | bytes 98304 | tf_op jit(solution)/shard_map/psum | solution.py:73
  127.4 95.2 %all-reduce.2.cloned.1.call-done = f32[128,256]{0,1:T(8,128)} async-done(((f32[128,256]{0,1:T(8,128)}), f32[128,256]{0,1:T(8,128)}) %all-reduce.2.cloned.1.call-update) | async-done | bytes 131088 | tf_op jit(solution)/shard_map/psum | solution.py:64
  222.6 0.9 fusion.19
  223.5 0.7 copy.24
  224.2 0.7 copy.25
  (15 shorter events, 0.1 us)
Async XLA Ops:
  7.2 13.9 %copy-start = (bf16[128,128]{1,0:T(8,128)(2,1)S(1)}, bf16[128,128]{1,0:T(8,128)(2,1)}, u32[]{:S(2)}) copy-start(bf16[128,128]{1,0:T(8,128)(2,1)} %param.7) | copy-start | bytes 98308
  11.2 9.9 %copy-start.2 = (bf16[128,128]{1,0:T(8,128)(2,1)S(1)}, bf16[128,128]{1,0:T(8,128)(2,1)}, u32[]{:S(2)}) copy-start(bf16[128,128]{1,0:T(8,128)(2,1)} %param.9) | copy-start | bytes 98308
  12.1 15.7 %all-to-all-start.1 = ((f32[16,1,256]{2,1,0:T(1,128)}), f32[16,1,256]{2,1,0:T(1,128)S(1)}, u32[]{:S(2)}, u32[]{:S(2)}) async-start(f32[16,1,256]{2,1,0:T(1,128)} %bitcast.5), calls=%async_computation.1 | async-start | bytes 32768 | tf_op jit(solution)/shard_map/all_to_all | solution.py:41
  23.0 8.5 %copy-start.3 = (bf16[128,128]{1,0:T(8,128)(2,1)S(1)}, bf16[128,128]{1,0:T(8,128)(2,1)}, u32[]{:S(2)}) copy-start(bf16[128,128]{1,0:T(8,128)(2,1)} %param.13) | copy-start | bytes 98308
  23.0 8.6 %copy-start.1 = (bf16[16,128,128]{2,1,0:T(8,128)(2,1)S(1)}, bf16[16,128,128]{2,1,0:T(8,128)(2,1)}, u32[]{:S(2)}) copy-start(bf16[16,128,128]{2,1,0:T(8,128)(2,1)} %param.10) | copy-start | bytes 1572868
  23.0 8.7 %copy-start.5 = (s32[16,1]{0,1:T(1,128)S(1)}, s32[16,1]{0,1:T(1,128)}, u32[]{:S(2)}) copy-start(s32[16,1]{0,1:T(1,128)} %param.11) | copy-start | bytes 196
  23.0 9.2 %copy-start.6 = (s32[128]{0:T(128)S(1)}, s32[128]{0:T(128)}, u32[]{:S(2)}) copy-start(s32[128]{0:T(128)} %param.12) | copy-start | bytes 1540
  27.7 46.0 %all-to-all-start = ((f32[16,256,128]{2,1,0:T(8,128)}), f32[16,256,128]{2,1,0:T(8,128)S(1)}, u32[]{:S(2)}, u32[]{:S(2)}) async-start(f32[16,256,128]{2,1,0:T(8,128)} %fusion.2), calls=%async_computation | async-start | bytes 4194304 | tf_op jit(solution)/shard_map/all_to_all | solution.py:40
  31.5 42.4 %copy-start.4 = (bf16[128,128]{1,0:T(8,128)(2,1)S(1)}, bf16[128,128]{1,0:T(8,128)(2,1)}, u32[]{:S(2)}) copy-start(bf16[128,128]{1,0:T(8,128)(2,1)} %param.8) | copy-start | bytes 98308
  31.5 191.1 %all-reduce.2.cloned.1.call-start = ((), (), s32[]{:S(2)}) async-start(), calls=%async_computation.2 | async-start | bytes 262144 | tf_op jit(solution)/shard_map/psum | solution.py:64
Sparse Core Ops, SparseCore 0:
  122.5 100.1 all-reduce.1
where the time goes:
time: 232 us
  waiting for transfers between devices  141 us (61%)
  blocking collectives  51 us (22%)
  between operations  14.2 us (6%)
  starting transfers between devices  12.1 us (5%)
  matrix products  5.6 us (2%)
  local copies, waits for them, and re-layouts  4.2 us (2%)
  other arithmetic  3.27 us (1%)
    psum x1, waiting for transfers between devices, on_device(): weight_sum = lax.psum(local_term, 'dom')  95.2 us
    all_gather x1, blocking collectives, on_device(): lax.all_gather(dagg, 'dom', axis=0, tiled=True)  46.9 us
    all_to_all x1, waiting for transfers between devices, on_device(): lax.all_to_all(partial_sums, 'dom', split_axis=0, concat_axis=0, tiled=True)  41.5 us
    all_to_all x1, starting transfers between devices, on_device(): lax.all_to_all(slot_links, 'dom', split_axis=0, concat_axis=0, tiled=True)  8.31 us
    all_to_all x1, waiting for transfers between devices, on_device(): lax.all_to_all(slot_links, 'dom', split_axis=0, concat_axis=0, tiled=True)  4.72 us
  transfers between devices with their start and end apart: 3, of which 3 were waited for; matrix products, arithmetic and copies ran while one was open for 2% of the time, Pallas kernels for 0%

commit v1 on v0

v1 whole, which is shorter than its diff:
```python
import jax
import jax.numpy as jnp
from jax import lax
from jax.experimental import pallas as pl
from jax.experimental.pallas import tpu as pltpu
from jax.sharding import PartitionSpec as P

BF16 = jnp.bfloat16
F32 = jnp.float32
EXTRA = 8
MIB = 1 << 20

NN = (((1,), (0,)), ((), ()))
NT = (((1,), (1,)), ((), ()))


def dot(a, b, dims):
    return lax.dot_general(a, b, dims, preferred_element_type=F32)


def loop(count, body):
    if count <= 16:
        for index in range(count):
            body(index)
    else:
        pl.loop(0, count)(body)


def listed(index, peers):
    bits = peers.bit_length() - 1
    index = index ^ (peers - 1)
    return sum(((index >> bit) & 1) << (bits - 1 - bit) for bit in range(bits))


def halves(size):
    core = lax.axis_index("feat")
    half = size // 2
    return pl.ds(pl.multiple_of(core * half, half), half), pl.ds(pl.multiple_of((1 - core) * half, half), half)


def share_kernel(
    dest_hbm, features_hbm, tiles_hbm, share_ref, dest_ref, features_ref, tiles_ref, turned_ref, sums_ref, sems,
):
    copies = [
        pltpu.make_async_copy(source, target, sems.at[i])
        for i, (source, target) in enumerate(
            [(features_hbm, features_ref), (dest_hbm, dest_ref), (tiles_hbm, tiles_ref)]
        )
    ]
    for copy in copies:
        copy.start()
    peers = sums_ref.shape[0]
    sums_ref[...] = jnp.zeros_like(sums_ref)
    copies[0].wait()
    turned_ref[...] = features_ref[...].T
    own, _ = halves(turned_ref.shape[0])
    left = jnp.concatenate([turned_ref[own, :], jnp.ones((EXTRA, turned_ref.shape[1]), BF16)], axis=0)
    copies[1].wait()
    copies[2].wait()

    def add(t):
        sums_ref[listed(dest_ref[t], peers)] += dot(left, tiles_ref[t], NN)

    loop(tiles_ref.shape[0], add)
    share_ref[...] = sums_ref[...].astype(BF16)


def sum_kernel(arrived_ref, w_self_ref, w_neigh_ref, cotangent_ref, total_ref, links_ref):
    half = arrived_ref.shape[1] - EXTRA
    fin = w_self_ref.shape[0]
    total = jnp.sum(arrived_ref[...].astype(F32), axis=0)
    links_ref[...] = total[half:]
    total_ref[:half] = total[:half].astype(BF16)
    total_ref[half : half + fin] = w_self_ref[...]
    total_ref[half + fin : half + 2 * fin] = w_neigh_ref[...]
    _, sibling = halves(cotangent_ref.shape[0])
    total_ref[half + 2 * fin :] = cotangent_ref[sibling, :]


def node_kernel(
    total_ref, other_ref, links_ref, outside_ref, features_ref, w_self_ref, w_neigh_ref, cotangent_ref,
    output_ref, packed_ref, term_ref, gathered_ref, nodes_ref, scale_ref, dagg_ref,
):
    fin, rows = gathered_ref.shape
    hidden = w_self_ref.shape[1]
    quarter = fin // 2
    own, sibling = halves(fin)
    low, _ = halves(rows)
    gathered_ref[own, :] = total_ref[:quarter]
    gathered_ref[sibling, :] = other_ref[:quarter]
    gathered = gathered_ref[...]
    nodes_ref[...] = gathered.T
    degree = links_ref[0:1] + outside_ref[...].astype(F32)
    scale_ref[...] = jnp.broadcast_to(1.0 / degree, (hidden, rows)).T

    def gradients(features, nodes, scale, w_self, w_neigh, cotangent):
        pre = dot(features, w_self, NN) + dot(nodes, w_neigh, NN) * scale
        sigma = 1.0 / (1.0 + jnp.exp(-pre))
        dpre = (cotangent.astype(F32) * sigma * (1.0 + pre * (1.0 - sigma))).astype(BF16)
        return pre * sigma, dpre, (dpre.astype(F32) * scale).astype(BF16)

    features, w_neigh = features_ref[...], w_neigh_ref[...]
    silu, dpre, dagg = gradients(
        features, nodes_ref[...], scale_ref[...], w_self_ref[...], w_neigh, cotangent_ref[...]
    )
    output_ref[...] = silu.astype(BF16)
    dagg_ref[...] = dagg
    w_self_other = other_ref[quarter : quarter + fin]
    w_neigh_other = other_ref[quarter + fin : quarter + 2 * fin]
    _, _, dagg_other = gradients(
        features_ref[low, :], nodes_ref[low, :], scale_ref[low, :], w_self_other, w_neigh_other,
        other_ref[quarter + 2 * fin :],
    )
    back = dot(dagg_ref[low, :], w_neigh, NT) + dot(dagg_other, w_neigh_other, NT)
    peers, packed, _ = packed_ref.shape
    slab = 2 * fin // peers
    half = rows // 2
    packed_ref[:, :half] = jnp.broadcast_to(back.astype(BF16)[None], (peers, half, fin))
    weight = jnp.concatenate([dot(features.T, dpre, NN), dot(gathered, dagg, NN)], axis=0)
    weight = weight.reshape(peers, slab, hidden)
    if packed - half > slab:
        weight = jnp.concatenate([weight, jnp.zeros((peers, packed - half - slab, hidden), F32)], axis=1)
    packed_ref[:, half:] = weight.astype(BF16)
    term_ref[...] = dot(dpre, w_self_ref[...], NT)


def input_kernel(dest_ref, back_ref, tiles_ref, term_ref, total_ref, padded_ref):
    own, sibling = halves(tiles_ref.shape[2])
    half = tiles_ref.shape[2] // 2
    peers = padded_ref.shape[0]
    padded_ref[:, own, :] = back_ref[:, :half]
    padded_ref[:, sibling, :] = jnp.zeros((padded_ref.shape[0], half, padded_ref.shape[2]), BF16)
    total = term_ref[...]
    if tiles_ref.shape[0] <= 16:
        for t in range(tiles_ref.shape[0]):
            total = total + dot(tiles_ref[t], padded_ref[listed(dest_ref[t], peers)], NN)
    else:
        total = lax.fori_loop(
            0, tiles_ref.shape[0], lambda t, sum: sum + dot(tiles_ref[t], padded_ref[listed(dest_ref[t], peers)], NN), total
        )
    total_ref[...] = total


def spread_kernel(part_ref, parts_ref):
    parts_ref[...] = jnp.broadcast_to(part_ref[...][None], parts_ref.shape)


def output_kernel(silu_ref, term_ref, other_ref, weight_ref, output_ref, grad_input_ref, grad_self_ref, grad_neigh_ref):
    output_ref[...] = silu_ref[...]
    fin = grad_self_ref.shape[0]
    grad_input_ref[...] = (term_ref[...] + other_ref[...]).astype(BF16)
    grad_self_ref[...] = weight_ref[:fin].astype(F32)
    grad_neigh_ref[...] = weight_ref[fin:].astype(F32)


def on_device(features, w_self, w_neigh, tiles, dest, outside, cotangent):
    peers = lax.axis_size("dom")
    tile_count, rows, _ = tiles.shape
    fin, hidden = w_self.shape
    half = fin // 2
    slab = 2 * fin // peers
    smem = pl.BlockSpec(memory_space=pltpu.SMEM)
    vmem = pl.BlockSpec(memory_space=pltpu.VMEM)
    hbm = pl.BlockSpec(memory_space=pltpu.HBM)
    targets = dest.reshape(-1)
    shape = jax.ShapeDtypeStruct

    def swap(x):
        return lax.ppermute(x, "feat", [(0, 1), (1, 0)])

    group = sorted(range(peers), key=lambda index: listed(index, peers))

    def exchange(x):
        return lax.all_to_all(x, "dom", split_axis=0, concat_axis=0, tiled=True, axis_index_groups=[group])

    extended = half + EXTRA
    share = pl.pallas_call(
        share_kernel,
        out_shape=pltpu.VMEM((peers, extended, rows), BF16),
        in_specs=[hbm] * 3,
        out_specs=vmem,
        scratch_shapes=[
            pltpu.SMEM((tile_count,), jnp.int32),
            pltpu.VMEM((rows, fin), BF16),
            pltpu.VMEM(tiles.shape, BF16),
            pltpu.VMEM((fin, rows), BF16),
            pltpu.VMEM((peers, extended, rows), F32),
            pltpu.SemaphoreType.DMA((3,)),
        ],
        compiler_params=pltpu.CompilerParams(vmem_limit_bytes=60 * MIB),
        name="share",
    )(targets, features, tiles)
    arrived = exchange(share)
    together = half + 2 * fin + rows // 2
    total, links = pl.pallas_call(
        sum_kernel,
        out_shape=(pltpu.VMEM((together, hidden), BF16), pltpu.VMEM((EXTRA, rows), F32)),
        in_specs=[vmem] * 4,
        out_specs=(vmem,) * 2,
        compiler_params=pltpu.CompilerParams(vmem_limit_bytes=(4 + peers // 8) * MIB),
        name="sum",
    )(arrived, w_self, w_neigh, cotangent)
    output, packed, term = pl.pallas_call(
        node_kernel,
        out_shape=(
            pltpu.VMEM((rows, hidden), BF16),
            pltpu.VMEM((peers, rows // 2 + max(slab, 16), hidden), BF16),
            shape((rows, fin), F32),
        ),
        in_specs=[vmem] * 8,
        out_specs=(vmem,) * 3,
        scratch_shapes=[
            pltpu.VMEM((fin, rows), BF16),
            pltpu.VMEM((rows, fin), BF16),
            pltpu.VMEM((rows, hidden), F32),
            pltpu.VMEM((rows, hidden), BF16),
        ],
        compiler_params=pltpu.CompilerParams(vmem_limit_bytes=(4 + peers // 8) * MIB),
        name="node",
    )(total, swap(total), links, outside.reshape(1, rows), features, w_self, w_neigh, cotangent)
    back = exchange(packed)
    summed = jnp.sum(back[:, rows // 2 : rows // 2 + slab].astype(F32), axis=0).astype(BF16)
    summed = pl.pallas_call(
        spread_kernel,
        out_shape=pltpu.VMEM((peers, slab, hidden), BF16),
        in_specs=[vmem],
        out_specs=vmem,
        compiler_params=pltpu.CompilerParams(vmem_limit_bytes=4 * MIB),
        name="spread",
    )(summed)
    summed, back = lax.optimization_barrier((summed, back))
    weight = exchange(summed)
    term = pl.pallas_call(
        input_kernel,
        out_shape=shape((rows, fin), F32),
        in_specs=[smem] + [vmem] * 3,
        out_specs=vmem,
        scratch_shapes=[pltpu.VMEM((peers, rows, fin), BF16)],
        compiler_params=pltpu.CompilerParams(vmem_limit_bytes=(4 + peers // 8) * MIB),
        name="input",
    )(targets, back, tiles, term)
    block = shape((fin, hidden), F32)
    return pl.pallas_call(
        output_kernel,
        out_shape=(shape((rows, hidden), BF16), shape((rows, fin), BF16), block, block),
        in_specs=[vmem] * 4,
        out_specs=(vmem,) * 4,
        compiler_params=pltpu.CompilerParams(vmem_limit_bytes=4 * MIB),
        name="outputs",
    )(output, term, swap(term), weight.reshape(2 * fin, hidden))


def solution(mesh):
    placed = (
        P("dom", None),
        P(None, "feat"),
        P(None, "feat"),
        P("dom", None, None),
        P("dom", None),
        P("dom"),
        P("dom", "feat"),
    )
    return jax.shard_map(
        on_device,
        mesh=mesh,
        in_specs=placed,
        out_specs=(P("dom", "feat"), P("dom", None), P(None, "feat"), P(None, "feat")),
        check_vma=False,
    )
```

time: 232 us -> 47.9 us (0.21)
  waiting for transfers between devices: 141 us -> 2.53 us
  blocking collectives: 51 us -> 31.7 us
  between operations: 14.2 us -> 0.74 us
  matrix products: 5.6 us -> 0 us
  starting transfers between devices: 12.1 us -> 7.07 us
  Pallas kernels: 0 us -> 4.16 us
  other arithmetic: 3.27 us -> 0.02 us
  local copies, waits for them, and re-layouts: 4.2 us -> 1.32 us
    psum x1 -> x0, waiting for transfers between devices: 95.2 us -> none  [on_device(): weight_sum = lax.psum(local_term, 'dom')]
    all_gather x1 -> x0, blocking collectives: 46.9 us -> none  [on_device(): lax.all_gather(dagg, 'dom', axis=0, tiled=True)]
    all_to_all x2 -> x1, waiting for transfers between devices: 46.2 us -> 0.01 us  [exchange(): lax.all_to_all(x, 'dom', split_axis=0, concat_axis=0, tiled=True, axis_in...]
    all_to_all x0 -> x2, blocking collectives: none -> 31.7 us  [exchange(): lax.all_to_all(x, 'dom', split_axis=0, concat_axis=0, tiled=True, axis_in...]
    dot_general x8 -> x0, matrix products: 5.6 us -> none  [the longest x1 1.91 us: on_device(): jnp.einsum('sij,ik->sjk', slot_tiles, message, preferred_element_type=jnp...]
    all_to_all x2 -> x1, starting transfers between devices: 12 us -> 6.92 us  [exchange(): lax.all_to_all(x, 'dom', split_axis=0, concat_axis=0, tiled=True, axis_in...]
    pallas_call x0 -> x6, Pallas kernels: none -> 4.16 us  [the longest x1 1.45 us: on_device(): pl.pallas_call(share_kernel, out_shape=pltpu.VMEM((peers, extended, rows)...]
    psum x1 -> x0, blocking collectives: 4.15 us -> none  [on_device(): grad_input = lax.psum(input_term, 'feat').astype(jnp.bfloat16)]
  transfers between devices with their start and end apart: 3 -> 3, of which waited for: 3 -> 2; matrix products, arithmetic and copies ran while one was open for 2% -> 0% of each run, Pallas kernels for 0% -> 2%
where the time goes in v1:
time: 47.9 us; the launch traced here: 47.5 us
  blocking collectives  31.7 us (66%)
  starting transfers between devices  7.07 us (15%)
  Pallas kernels  4.16 us (9%)
  waiting for transfers between devices  2.53 us (5%)
  local copies, waits for them, and re-layouts  1.32 us (3%)
  between operations  0.74 us (2%)
    all_to_all x2, blocking collectives, exchange(): lax.all_to_all(x, 'dom', split_axis=0, concat_axis=0, tiled=True, axis_in...  31.7 us
    all_to_all x1, starting transfers between devices, exchange(): lax.all_to_all(x, 'dom', split_axis=0, concat_axis=0, tiled=True, axis_in...  6.92 us
    ppermute x2, waiting for transfers between devices, swap(): return lax.ppermute(x, 'feat', [(0, 1), (1, 0)])  2.53 us
    pallas_call x1, Pallas kernels, on_device(): pl.pallas_call(share_kernel, out_shape=pltpu.VMEM((peers, extended, rows)...  1.45 us
    unnamed x14, local copies, waits for them, and re-layouts  1.32 us
  transfers between devices with their start and end apart: 3, of which 2 were waited for; matrix products, arithmetic and copies ran while one was open for 0% of the time, Pallas kernels for 2%

profile of v1, /device:TPU:0, one launch (start us, length us, event | category | flops | bytes accessed | tf_op | source)
XLA Modules:
  0.0 47.5 jit_solution(17660407746970229167)
XLA Ops:
  0.6 1.5 %share.1 = bf16[16,72,128]{2,1,0:T(8,128)(2,1)S(1)} custom-call(s32[16]{0:T(128)} %bitcast.4, bf16[128,128]{1,0:T(8,128)(2,1)} %features_ref.1, bf16[16,128,128]{2,1,0:T(8,128)(2,1)} %tiles_ref.1), custom_call_target="tpu_custom_call" | custom-call | tf_op jit(solution)/shard_map/share/pallas_call | solution.py:177
  2.1 0.0 copy-start.2
  2.1 0.0 copy-start.3
  2.1 0.0 copy-start.4
  2.1 16.8 %all_to_all.15.arrived_ref = bf16[16,72,128]{2,1,0:T(8,128)(2,1)S(1)} all-to-all(bf16[16,72,128]{2,1,0:T(8,128)(2,1)S(1)} %share.1), channel_id=1, replica_groups={{30,14,22,6,26,10,18,2,28,12,20,4,24,8,16,0},{31,15,23,7,27,11,19,3,29,..., dimensions={0} | all-to-all | bytes 589824 | tf_op jit(solution)/shard_map/all_to_all | solution.py:174
  18.9 0.0 copy-done.2
  18.9 0.0 copy-done.3
  18.9 0.0 copy-done.4
  18.9 0.0 copy-start.1
  19.0 0.1 collective-permute-start
  19.1 1.3 %collective-permute-done.other_ref = bf16[384,128]{1,0:T(8,128)(2,1)S(1)} collective-permute-done((bf16[384,128]{1,0:T(8,128)(2,1)S(1)}, bf16[384,128]{1,0:T(8,128)(2,1)S(1)}, u32[]{:S(2)}, u32[]{:S(2)}) %collective-permute-start) | collective-permute-done | bytes 98336 | tf_op jit(solution)/shard_map/ppermute | solution.py:169
  20.3 0.0 copy-start.6
  20.3 0.0 copy-done.1
  20.4 0.7 %copy-done.6 = s32[128]{0:T(128)S(1)} copy-done((s32[128]{0:T(128)S(1)}, s32[128]{0:T(128)}, u32[]{:S(2)}) %copy-start.6) | copy-done | bytes 536
  21.0 0.4 node.1
  21.4 0.0 copy-start
  21.5 14.9 %all_to_all.16.back_ref = bf16[16,80,128]{2,1,0:T(8,128)(2,1)S(1)} all-to-all(bf16[16,80,128]{2,1,0:T(8,128)(2,1)S(1)} %get-tuple-element.14), channel_id=1, replica_groups={{30,14,22,6,26,10,18,2,28,12,20,4,24,8,16,0},{31,15,23,7,27,11,19,3,29,..., dimensions={0} | all-to-all | bytes 655360 | tf_op jit(solution)/shard_map/all_to_all | solution.py:174
  36.4 0.6 %spread.1 = bf16[16,16,128]{2,1,0:T(8,128)(2,1)} custom-call(bf16[16,128]{1,0:T(8,128)(2,1)S(1)} %slice_reduce_fusion.part_ref), custom_call_target="tpu_custom_call" | custom-call | tf_op jit(solution)/shard_map/spread/pallas_call | solution.py:223
  37.1 6.9 %all-to-all-start.2 = ((bf16[16,16,128]{2,1,0:T(8,128)(2,1)}), bf16[16,16,128]{2,1,0:T(8,128)(2,1)S(1)}, u32[]{:S(2)}, u32[]{:S(2)}) async-start(bf16[16,16,128]{2,1,0:T(8,128)(2,1)} %spread.1), calls=%async_computation.2 | async-start | bytes 131072 | tf_op jit(solution)/shard_map/all_to_all | solution.py:174
  44.0 0.0 copy-start.5
  44.0 0.0 copy-done
  44.0 0.6 %copy-done.5 = s32[16,1]{0,1:T(1,128)S(1)} copy-done((s32[16,1]{0,1:T(1,128)S(1)}, s32[16,1]{0,1:T(1,128)}, u32[]{:S(2)}) %copy-start.5) | copy-done | bytes 88
  44.6 0.9 %input.1.term_ref = f32[128,128]{1,0:T(8,128)S(1)} custom-call(s32[16]{0:T(128)S(1)} %bitcast.5, bf16[16,80,128]{2,1,0:T(8,128)(2,1)S(1)} %all_to_all.16.back_ref, bf16[16,128,128]{2,1,0:T(8,128)(2,1)S(1)} %copy-done, f32[128,128]{1,0:T(8,128)S(1)} %get-tuple-element.16.term_ref), custom_call_target="tpu_custom_call" | custom-call | tf_op jit(solution)/shard_map/input/pallas_call | solution.py:233
  45.5 0.1 collective-permute-start.1
  45.6 1.2 %collective-permute-done.1.other_ref = f32[128,128]{1,0:T(8,128)S(1)} collective-permute-done((f32[128,128]{1,0:T(8,128)S(1)}, f32[128,128]{1,0:T(8,128)S(1)}, u32[]{:S(2)}, u32[]{:S(2)}) %collective-permute-start.1) | collective-permute-done | bytes 65568 | tf_op jit(solution)/shard_map/ppermute | solution.py:169
  46.9 0.0 all-to-all-done.2
  46.9 0.7 %outputs.1 = (bf16[128,128]{1,0:T(8,128)(2,1)}, bf16[128,128]{1,0:T(8,128)(2,1)}, f32[128,128]{1,0:T(8,128)}, f32[128,128]{1,0:T(8,128)}) custom-call(bf16[128,128]{1,0:T(8,128)(2,1)S(1)} %get-tuple-element.13.silu_ref, f32[128,128]{1,0:T(8,128)S(1)} %input.1.term_ref, f32[128,128]{1,0:T(8,128)S(1)} %collective-permute-done.1.other_ref, ...), custom_call_target="tpu_custom_call" | custom-call | tf_op jit(solution)/shard_map/outputs/pallas_call | solution.py:243
  (2 shorter events, 0.1 us)
Async XLA Ops:
  2.1 16.8 %copy-start.2 = (bf16[128,128]{1,0:T(8,128)(2,1)S(1)}, bf16[128,128]{1,0:T(8,128)(2,1)}, u32[]{:S(2)}) copy-start(bf16[128,128]{1,0:T(8,128)(2,1)} %w_self_ref.3) | copy-start | bytes 98308
  2.1 16.8 %copy-start.3 = (bf16[128,128]{1,0:T(8,128)(2,1)S(1)}, bf16[128,128]{1,0:T(8,128)(2,1)}, u32[]{:S(2)}) copy-start(bf16[128,128]{1,0:T(8,128)(2,1)} %w_neigh_ref.3) | copy-start | bytes 98308
  2.1 16.8 %copy-start.4 = (bf16[128,128]{1,0:T(8,128)(2,1)S(1)}, bf16[128,128]{1,0:T(8,128)(2,1)}, u32[]{:S(2)}) copy-start(bf16[128,128]{1,0:T(8,128)(2,1)} %cotangent_ref.3) | copy-start | bytes 98308
  18.9 1.4 %copy-start.1 = (bf16[128,128]{1,0:T(8,128)(2,1)S(1)}, bf16[128,128]{1,0:T(8,128)(2,1)}, u32[]{:S(2)}) copy-start(bf16[128,128]{1,0:T(8,128)(2,1)} %features_ref.1) | copy-start | bytes 98308
  19.0 1.4 %collective-permute-start = (bf16[384,128]{1,0:T(8,128)(2,1)S(1)}, bf16[384,128]{1,0:T(8,128)(2,1)S(1)}, u32[]{:S(2)}, u32[]{:S(2)}) collective-permute-start(bf16[384,128]{1,0:T(8,128)(2,1)S(1)} %get-tuple-element.11.total_ref), channel_id=1, source_target_pairs={{0,1},{1,0},{2,3},{3,2},{4,5},{5,4},{6,7},{7,6},{8,9},{9,8},{10,11... | collective-permute-start | bytes 294920 | tf_op jit(solution)/shard_map/ppermute | solution.py:169
  20.3 0.7 %copy-start.6 = (s32[128]{0:T(128)S(1)}, s32[128]{0:T(128)}, u32[]{:S(2)}) copy-start(s32[128]{0:T(128)} %param.12) | copy-start | bytes 1540
  21.4 22.5 %copy-start = (bf16[16,128,128]{2,1,0:T(8,128)(2,1)S(1)}, bf16[16,128,128]{2,1,0:T(8,128)(2,1)}, u32[]{:S(2)}) copy-start(bf16[16,128,128]{2,1,0:T(8,128)(2,1)} %tiles_ref.1) | copy-start | bytes 1572868
  37.1 9.8 %all-to-all-start.2 = ((bf16[16,16,128]{2,1,0:T(8,128)(2,1)}), bf16[16,16,128]{2,1,0:T(8,128)(2,1)S(1)}, u32[]{:S(2)}, u32[]{:S(2)}) async-start(bf16[16,16,128]{2,1,0:T(8,128)(2,1)} %spread.1), calls=%async_computation.2 | async-start | bytes 131072 | tf_op jit(solution)/shard_map/all_to_all | solution.py:174
  44.0 0.7 %copy-start.5 = (s32[16,1]{0,1:T(1,128)S(1)}, s32[16,1]{0,1:T(1,128)}, u32[]{:S(2)}) copy-start(s32[16,1]{0,1:T(1,128)} %param.11) | copy-start | bytes 196
  45.5 1.3 %collective-permute-start.1 = (f32[128,128]{1,0:T(8,128)S(1)}, f32[128,128]{1,0:T(8,128)S(1)}, u32[]{:S(2)}, u32[]{:S(2)}) collective-permute-start(f32[128,128]{1,0:T(8,128)S(1)} %input.1.term_ref), channel_id=1, source_target_pairs={{0,1},{1,0},{2,3},{3,2},{4,5},{5,4},{6,7},{7,6},{8,9},{9,8},{10,11... | collective-permute-start | bytes 196616 | tf_op jit(solution)/shard_map/ppermute | solution.py:169

commit v2 on v1

--- a/solution.py
+++ b/solution.py
@@ -28,7 +28,7 @@
 
 def listed(index, peers):
     bits = peers.bit_length() - 1
-    index = index ^ (peers - 1)
+    index = index ^ (peers - peers // 4 - 1)
     return sum(((index >> bit) & 1) << (bits - 1 - bit) for bit in range(bits))
 
 
@@ -39,12 +39,12 @@
 
 
 def share_kernel(
-    dest_hbm, features_hbm, tiles_hbm, share_ref, dest_ref, features_ref, tiles_ref, turned_ref, sums_ref, sems,
+    dest_hbm, features_hbm, outside_hbm, tiles_hbm, share_ref, outside_ref, dest_ref, features_ref, tiles_ref, turned_ref, sums_ref, sems,
 ):
     copies = [
         pltpu.make_async_copy(source, target, sems.at[i])
         for i, (source, target) in enumerate(
-            [(features_hbm, features_ref), (dest_hbm, dest_ref), (tiles_hbm, tiles_ref)]
+            [(features_hbm, features_ref), (dest_hbm, dest_ref), (tiles_hbm, tiles_ref), (outside_hbm, outside_ref)]
         )
     ]
     for copy in copies:
@@ -63,6 +63,7 @@
 
     loop(tiles_ref.shape[0], add)
     share_ref[...] = sums_ref[...].astype(BF16)
+    copies[3].wait()
 
 
 def sum_kernel(arrived_ref, w_self_ref, w_neigh_ref, cotangent_ref, total_ref, links_ref):
@@ -174,22 +175,22 @@
         return lax.all_to_all(x, "dom", split_axis=0, concat_axis=0, tiled=True, axis_index_groups=[group])
 
     extended = half + EXTRA
-    share = pl.pallas_call(
+    share, outside = pl.pallas_call(
         share_kernel,
-        out_shape=pltpu.VMEM((peers, extended, rows), BF16),
-        in_specs=[hbm] * 3,
-        out_specs=vmem,
+        out_shape=(pltpu.VMEM((peers, extended, rows), BF16), pltpu.VMEM((1, rows), jnp.int32)),
+        in_specs=[hbm] * 4,
+        out_specs=(vmem, vmem),
         scratch_shapes=[
             pltpu.SMEM((tile_count,), jnp.int32),
             pltpu.VMEM((rows, fin), BF16),
             pltpu.VMEM(tiles.shape, BF16),
             pltpu.VMEM((fin, rows), BF16),
             pltpu.VMEM((peers, extended, rows), F32),
-            pltpu.SemaphoreType.DMA((3,)),
+            pltpu.SemaphoreType.DMA((4,)),
         ],
         compiler_params=pltpu.CompilerParams(vmem_limit_bytes=60 * MIB),
         name="share",
-    )(targets, features, tiles)
+    )(targets, features, outside.reshape(1, rows), tiles)
     arrived = exchange(share)
     together = half + 2 * fin + rows // 2
     total, links = pl.pallas_call(
@@ -217,7 +218,7 @@
         ],
         compiler_params=pltpu.CompilerParams(vmem_limit_bytes=(4 + peers // 8) * MIB),
         name="node",
-    )(total, swap(total), links, outside.reshape(1, rows), features, w_self, w_neigh, cotangent)
+    )(total, swap(total), links, outside, features, w_self, w_neigh, cotangent)
     back = exchange(packed)
     summed = jnp.sum(back[:, rows // 2 : rows // 2 + slab].astype(F32), axis=0).astype(BF16)
     summed = pl.pallas_call(

time: 47.9 us -> 45.7 us (0.954)
  blocking collectives: 31.7 us -> 29.8 us
  waiting for transfers between devices: 2.53 us -> 3.34 us
  local copies, waits for them, and re-layouts: 1.32 us -> 0.67 us
    all_to_all x2, blocking collectives: 31.7 us -> 29.8 us  [exchange(): lax.all_to_all(x, 'dom', split_axis=0, concat_axis=0, tiled=True, axis_in...]
    all_to_all x1, waiting for transfers between devices: 0.01 us -> 0.81 us  [exchange(): lax.all_to_all(x, 'dom', split_axis=0, concat_axis=0, tiled=True, axis_in...]
    unnamed x14 -> x12, local copies, waits for them, and re-layouts: 1.32 us -> 0.67 us
  transfers between devices with their start and end apart: 3 -> 3, of which waited for: 2 -> 3; matrix products, arithmetic and copies ran while one was open for 0% -> 0% of each run, Pallas kernels for 2% -> 2%
where the time goes in v2:
time: 45.7 us; the launch traced here: 45.3 us
  blocking collectives  29.8 us (65%)
  starting transfers between devices  6.62 us (14%)
  Pallas kernels  4.17 us (9%)
  waiting for transfers between devices  3.34 us (7%)
  between operations  0.74 us (2%)
  local copies, waits for them, and re-layouts  0.67 us (1%)
    all_to_all x2, blocking collectives, exchange(): lax.all_to_all(x, 'dom', split_axis=0, concat_axis=0, tiled=True, axis_in...  29.8 us
    all_to_all x1, starting transfers between devices, exchange(): lax.all_to_all(x, 'dom', split_axis=0, concat_axis=0, tiled=True, axis_in...  6.48 us
    ppermute x2, waiting for transfers between devices, swap(): return lax.ppermute(x, 'feat', [(0, 1), (1, 0)])  2.53 us
    pallas_call x1, Pallas kernels, on_device(): pl.pallas_call(share_kernel, out_shape=(pltpu.VMEM((peers, extended, rows...  1.46 us
  transfers between devices with their start and end apart: 3, of which 3 were waited for; matrix products, arithmetic and copies ran while one was open for 0% of the time, Pallas kernels for 2%

profile of v2, /device:TPU:0, one launch (start us, length us, event | category | flops | bytes accessed | tf_op | source)
XLA Modules:
  0.0 45.3 jit_solution(2418768149683682408)
XLA Ops:
  0.6 1.5 %share.1 = (bf16[16,72,128]{2,1,0:T(8,128)(2,1)S(1)}, s32[1,128]{1,0:T(1,128)S(1)}) custom-call(s32[16]{0:T(128)} %bitcast.4, bf16[128,128]{1,0:T(8,128)(2,1)} %features_ref.1, s32[1,128]{1,0:T(1,128)} %bitcast.6, bf16[16,128,128]{2,1,0:T(8,128)(2,1)} %tiles_ref.1), custom_call_target="tpu_custom_call" | custom-call | tf_op jit(solution)/shard_map/share/pallas_call | solution.py:178
  2.1 0.0 copy-start.2
  2.1 0.0 copy-start.3
  2.1 0.0 copy-start.4
  2.1 15.7 %all_to_all.15.arrived_ref = bf16[16,72,128]{2,1,0:T(8,128)(2,1)S(1)} all-to-all(bf16[16,72,128]{2,1,0:T(8,128)(2,1)S(1)} %get-tuple-element.13), channel_id=1, replica_groups={{22,6,30,14,18,2,26,10,20,4,28,12,16,0,24,8},{23,7,31,15,19,3,27,11,21,..., dimensions={0} | all-to-all | bytes 589824 | tf_op jit(solution)/shard_map/all_to_all | solution.py:175
  17.8 0.0 copy-done.2
  17.8 0.0 copy-done.3
  17.8 0.0 copy-done.4
  17.8 0.0 copy-start.1
  17.9 0.1 collective-permute-start
  17.9 1.3 %collective-permute-done.other_ref = bf16[384,128]{1,0:T(8,128)(2,1)S(1)} collective-permute-done((bf16[384,128]{1,0:T(8,128)(2,1)S(1)}, bf16[384,128]{1,0:T(8,128)(2,1)S(1)}, u32[]{:S(2)}, u32[]{:S(2)}) %collective-permute-start) | collective-permute-done | bytes 98336 | tf_op jit(solution)/shard_map/ppermute | solution.py:170
  19.2 0.0 copy-done.1
  19.2 0.4 node.1
  19.7 0.0 copy-start
  19.7 14.1 %all_to_all.16.back_ref = bf16[16,80,128]{2,1,0:T(8,128)(2,1)S(1)} all-to-all(bf16[16,80,128]{2,1,0:T(8,128)(2,1)S(1)} %get-tuple-element.18), channel_id=1, replica_groups={{22,6,30,14,18,2,26,10,20,4,28,12,16,0,24,8},{23,7,31,15,19,3,27,11,21,..., dimensions={0} | all-to-all | bytes 655360 | tf_op jit(solution)/shard_map/all_to_all | solution.py:175
  33.8 0.6 %spread.1 = bf16[16,16,128]{2,1,0:T(8,128)(2,1)} custom-call(bf16[16,128]{1,0:T(8,128)(2,1)S(1)} %slice_reduce_fusion.part_ref), custom_call_target="tpu_custom_call" | custom-call | tf_op jit(solution)/shard_map/spread/pallas_call | solution.py:224
  34.5 6.5 %all-to-all-start.2 = ((bf16[16,16,128]{2,1,0:T(8,128)(2,1)}), bf16[16,16,128]{2,1,0:T(8,128)(2,1)S(1)}, u32[]{:S(2)}, u32[]{:S(2)}) async-start(bf16[16,16,128]{2,1,0:T(8,128)(2,1)} %spread.1), calls=%async_computation.2 | async-start | bytes 131072 | tf_op jit(solution)/shard_map/all_to_all | solution.py:175
  41.0 0.0 copy-start.5
  41.0 0.0 copy-done
  41.0 0.6 %copy-done.5 = s32[16,1]{0,1:T(1,128)S(1)} copy-done((s32[16,1]{0,1:T(1,128)S(1)}, s32[16,1]{0,1:T(1,128)}, u32[]{:S(2)}) %copy-start.5) | copy-done | bytes 88
  41.6 0.9 %input.1.term_ref = f32[128,128]{1,0:T(8,128)S(1)} custom-call(s32[16]{0:T(128)S(1)} %bitcast.5, bf16[16,80,128]{2,1,0:T(8,128)(2,1)S(1)} %all_to_all.16.back_ref, bf16[16,128,128]{2,1,0:T(8,128)(2,1)S(1)} %copy-done, f32[128,128]{1,0:T(8,128)S(1)} %get-tuple-element.20.term_ref), custom_call_target="tpu_custom_call" | custom-call | tf_op jit(solution)/shard_map/input/pallas_call | solution.py:234
  42.5 0.1 collective-permute-start.1
  42.6 1.2 %collective-permute-done.1.other_ref = f32[128,128]{1,0:T(8,128)S(1)} collective-permute-done((f32[128,128]{1,0:T(8,128)S(1)}, f32[128,128]{1,0:T(8,128)S(1)}, u32[]{:S(2)}, u32[]{:S(2)}) %collective-permute-start.1) | collective-permute-done | bytes 65568 | tf_op jit(solution)/shard_map/ppermute | solution.py:170
  43.8 0.8 %all-to-all-done.2 = bf16[16,16,128]{2,1,0:T(8,128)(2,1)S(1)} async-done(((bf16[16,16,128]{2,1,0:T(8,128)(2,1)}), bf16[16,16,128]{2,1,0:T(8,128)(2,1)S(1)}, u32[]{:S(2)}, u32[]{:S(2)}) %all-to-all-start.2) | async-done | bytes 65568 | tf_op jit(solution)/shard_map/all_to_all | solution.py:175
  44.6 0.7 %outputs.1 = (bf16[128,128]{1,0:T(8,128)(2,1)}, bf16[128,128]{1,0:T(8,128)(2,1)}, f32[128,128]{1,0:T(8,128)}, f32[128,128]{1,0:T(8,128)}) custom-call(bf16[128,128]{1,0:T(8,128)(2,1)S(1)} %get-tuple-element.17.silu_ref, f32[128,128]{1,0:T(8,128)S(1)} %input.1.term_ref, f32[128,128]{1,0:T(8,128)S(1)} %collective-permute-done.1.other_ref, ...), custom_call_target="tpu_custom_call" | custom-call | tf_op jit(solution)/shard_map/outputs/pallas_call | solution.py:244
  (2 shorter events, 0.1 us)
Async XLA Ops:
  2.1 15.7 %copy-start.2 = (bf16[128,128]{1,0:T(8,128)(2,1)S(1)}, bf16[128,128]{1,0:T(8,128)(2,1)}, u32[]{:S(2)}) copy-start(bf16[128,128]{1,0:T(8,128)(2,1)} %w_self_ref.3) | copy-start | bytes 98308
  2.1 15.7 %copy-start.3 = (bf16[128,128]{1,0:T(8,128)(2,1)S(1)}, bf16[128,128]{1,0:T(8,128)(2,1)}, u32[]{:S(2)}) copy-start(bf16[128,128]{1,0:T(8,128)(2,1)} %w_neigh_ref.3) | copy-start | bytes 98308
  2.1 15.7 %copy-start.4 = (bf16[128,128]{1,0:T(8,128)(2,1)S(1)}, bf16[128,128]{1,0:T(8,128)(2,1)}, u32[]{:S(2)}) copy-start(bf16[128,128]{1,0:T(8,128)(2,1)} %cotangent_ref.3) | copy-start | bytes 98308
  17.8 1.4 %copy-start.1 = (bf16[128,128]{1,0:T(8,128)(2,1)S(1)}, bf16[128,128]{1,0:T(8,128)(2,1)}, u32[]{:S(2)}) copy-start(bf16[128,128]{1,0:T(8,128)(2,1)} %features_ref.1) | copy-start | bytes 98308
  17.9 1.4 %collective-permute-start = (bf16[384,128]{1,0:T(8,128)(2,1)S(1)}, bf16[384,128]{1,0:T(8,128)(2,1)S(1)}, u32[]{:S(2)}, u32[]{:S(2)}) collective-permute-start(bf16[384,128]{1,0:T(8,128)(2,1)S(1)} %get-tuple-element.14.total_ref), channel_id=1, source_target_pairs={{0,1},{1,0},{2,3},{3,2},{4,5},{5,4},{6,7},{7,6},{8,9},{9,8},{10,11... | collective-permute-start | bytes 294920 | tf_op jit(solution)/shard_map/ppermute | solution.py:170
  19.7 21.3 %copy-start = (bf16[16,128,128]{2,1,0:T(8,128)(2,1)S(1)}, bf16[16,128,128]{2,1,0:T(8,128)(2,1)}, u32[]{:S(2)}) copy-start(bf16[16,128,128]{2,1,0:T(8,128)(2,1)} %tiles_ref.1) | copy-start | bytes 1572868
  34.5 10.2 %all-to-all-start.2 = ((bf16[16,16,128]{2,1,0:T(8,128)(2,1)}), bf16[16,16,128]{2,1,0:T(8,128)(2,1)S(1)}, u32[]{:S(2)}, u32[]{:S(2)}) async-start(bf16[16,16,128]{2,1,0:T(8,128)(2,1)} %spread.1), calls=%async_computation.2 | async-start | bytes 131072 | tf_op jit(solution)/shard_map/all_to_all | solution.py:175
  41.0 0.7 %copy-start.5 = (s32[16,1]{0,1:T(1,128)S(1)}, s32[16,1]{0,1:T(1,128)}, u32[]{:S(2)}) copy-start(s32[16,1]{0,1:T(1,128)} %param.11) | copy-start | bytes 196
  42.5 1.3 %collective-permute-start.1 = (f32[128,128]{1,0:T(8,128)S(1)}, f32[128,128]{1,0:T(8,128)S(1)}, u32[]{:S(2)}, u32[]{:S(2)}) collective-permute-start(f32[128,128]{1,0:T(8,128)S(1)} %input.1.term_ref), channel_id=1, source_target_pairs={{0,1},{1,0},{2,3},{3,2},{4,5},{5,4},{6,7},{7,6},{8,9},{9,8},{10,11... | collective-permute-start | bytes 196616 | tf_op jit(solution)/shard_map/ppermute | solution.py:170

commit v3 on v2

--- a/solution.py
+++ b/solution.py
@@ -8,6 +8,7 @@
 BF16 = jnp.bfloat16
 F32 = jnp.float32
 EXTRA = 8
+SHARERS = 2
 MIB = 1 << 20
 
 NN = (((1,), (0,)), ((), ()))
@@ -26,9 +27,9 @@
         pl.loop(0, count)(body)
 
 
-def listed(index, peers):
+def listed(index, peers, corner=False):
     bits = peers.bit_length() - 1
-    index = index ^ (peers - peers // 4 - 1)
+    index = index ^ (peers - 1 if corner else peers - peers // 4 - 1)
     return sum(((index >> bit) & 1) << (bits - 1 - bit) for bit in range(bits))
 
 
@@ -39,12 +40,12 @@
 
 
 def share_kernel(
-    dest_hbm, features_hbm, outside_hbm, tiles_hbm, share_ref, outside_ref, dest_ref, features_ref, tiles_ref, turned_ref, sums_ref, sems,
+    dest_hbm, features_hbm, outside_hbm, tiles_hbm, share_ref, outside_ref, targets_ref, dest_ref, features_ref, tiles_ref, turned_ref, sums_ref, sems,
 ):
     copies = [
         pltpu.make_async_copy(source, target, sems.at[i])
         for i, (source, target) in enumerate(
-            [(features_hbm, features_ref), (dest_hbm, dest_ref), (tiles_hbm, tiles_ref), (outside_hbm, outside_ref)]
+            [(features_hbm, features_ref), (dest_hbm, dest_ref), (tiles_hbm, tiles_ref), (outside_hbm, outside_ref), (dest_hbm, targets_ref)]
         )
     ]
     for copy in copies:
@@ -64,6 +65,7 @@
     loop(tiles_ref.shape[0], add)
     share_ref[...] = sums_ref[...].astype(BF16)
     copies[3].wait()
+    copies[4].wait()
 
 
 def sum_kernel(arrived_ref, w_self_ref, w_neigh_ref, cotangent_ref, total_ref, links_ref):
@@ -114,24 +116,35 @@
     )
     back = dot(dagg_ref[low, :], w_neigh, NT) + dot(dagg_other, w_neigh_other, NT)
     peers, packed, _ = packed_ref.shape
-    slab = 2 * fin // peers
-    half = rows // 2
-    packed_ref[:, :half] = jnp.broadcast_to(back.astype(BF16)[None], (peers, half, fin))
+    owners = peers // SHARERS
+    slab = 2 * fin // owners
+    half = rows // 4
+    back = back.astype(BF16)
     weight = jnp.concatenate([dot(features.T, dpre, NN), dot(gathered, dagg, NN)], axis=0)
-    weight = weight.reshape(peers, slab, hidden)
+    weight = weight.reshape(owners, slab, hidden)
     if packed - half > slab:
-        weight = jnp.concatenate([weight, jnp.zeros((peers, packed - half - slab, hidden), F32)], axis=1)
-    packed_ref[:, half:] = weight.astype(BF16)
+        weight = jnp.concatenate([weight, jnp.zeros((owners, packed - half - slab, hidden), F32)], axis=1)
+    order = sorted(range(peers), key=lambda index: listed(index, peers))
+    for k, index in enumerate(order):
+        packed_ref[k, :half] = back[(index & 1) * half : (index & 1) * half + half]
+        packed_ref[k, half:] = weight[listed(index % owners, owners, corner=True)].astype(BF16)
     term_ref[...] = dot(dpre, w_self_ref[...], NT)
 
 
-def input_kernel(dest_ref, back_ref, tiles_ref, term_ref, total_ref, padded_ref):
-    own, sibling = halves(tiles_ref.shape[2])
+def input_kernel(targets_ref, back_ref, pair_ref, tiles_ref, term_ref, total_ref, dest_ref, padded_ref, sem):
+    copy = pltpu.make_async_copy(targets_ref, dest_ref, sem)
+    copy.start()
     half = tiles_ref.shape[2] // 2
+    _, sibling = halves(tiles_ref.shape[2])
+    quarter = half // 2
+    first = lax.axis_index("feat") * half
+    odd = lax.axis_index("dom") & 1
+    padded_ref[:, pl.ds(pl.multiple_of(first + odd * quarter, quarter), quarter), :] = back_ref[...]
+    padded_ref[:, pl.ds(pl.multiple_of(first + (1 - odd) * quarter, quarter), quarter), :] = pair_ref[...]
+    padded_ref[:, sibling, :] = jnp.zeros((padded_ref.shape[0], half, padded_ref.shape[2]), BF16)
     peers = padded_ref.shape[0]
-    padded_ref[:, own, :] = back_ref[:, :half]
-    padded_ref[:, sibling, :] = jnp.zeros((padded_ref.shape[0], half, padded_ref.shape[2]), BF16)
     total = term_ref[...]
+    copy.wait()
     if tiles_ref.shape[0] <= 16:
         for t in range(tiles_ref.shape[0]):
             total = total + dot(tiles_ref[t], padded_ref[listed(dest_ref[t], peers)], NN)
@@ -142,8 +155,11 @@
     total_ref[...] = total
 
 
-def spread_kernel(part_ref, parts_ref):
-    parts_ref[...] = jnp.broadcast_to(part_ref[...][None], parts_ref.shape)
+def spread_kernel(back_ref, parts_ref):
+    _, slab, _ = parts_ref.shape
+    half = back_ref.shape[2] // 4
+    part = jnp.sum(back_ref[:, half : half + slab].astype(F32), axis=0).astype(BF16)
+    parts_ref[...] = jnp.broadcast_to(part[None], parts_ref.shape)
 
 
 def output_kernel(silu_ref, term_ref, other_ref, weight_ref, output_ref, grad_input_ref, grad_self_ref, grad_neigh_ref):
@@ -159,8 +175,7 @@
     tile_count, rows, _ = tiles.shape
     fin, hidden = w_self.shape
     half = fin // 2
-    slab = 2 * fin // peers
-    smem = pl.BlockSpec(memory_space=pltpu.SMEM)
+    slab = 2 * fin // (peers // SHARERS)
     vmem = pl.BlockSpec(memory_space=pltpu.VMEM)
     hbm = pl.BlockSpec(memory_space=pltpu.HBM)
     targets = dest.reshape(-1)
@@ -169,29 +184,35 @@
     def swap(x):
         return lax.ppermute(x, "feat", [(0, 1), (1, 0)])
 
-    group = sorted(range(peers), key=lambda index: listed(index, peers))
-
-    def exchange(x):
-        return lax.all_to_all(x, "dom", split_axis=0, concat_axis=0, tiled=True, axis_index_groups=[group])
-
+    def exchange(x, groups):
+        return lax.all_to_all(x, "dom", split_axis=0, concat_axis=0, tiled=True, axis_index_groups=groups)
+
+    middle = [sorted(range(peers), key=lambda index: listed(index, peers))]
+    owners = peers // SHARERS
+    corner = sorted(range(owners), key=lambda index: listed(index, owners, corner=True))
+    corner = [[first + index for index in corner] for first in range(0, peers, owners)]
     extended = half + EXTRA
-    share, outside = pl.pallas_call(
+    share, outside, targets = pl.pallas_call(
         share_kernel,
-        out_shape=(pltpu.VMEM((peers, extended, rows), BF16), pltpu.VMEM((1, rows), jnp.int32)),
+        out_shape=(
+            pltpu.VMEM((peers, extended, rows), BF16),
+            pltpu.VMEM((1, rows), jnp.int32),
+            pltpu.VMEM((tile_count,), jnp.int32),
+        ),
         in_specs=[hbm] * 4,
-        out_specs=(vmem, vmem),
+        out_specs=(vmem,) * 3,
         scratch_shapes=[
             pltpu.SMEM((tile_count,), jnp.int32),
             pltpu.VMEM((rows, fin), BF16),
             pltpu.VMEM(tiles.shape, BF16),
             pltpu.VMEM((fin, rows), BF16),
             pltpu.VMEM((peers, extended, rows), F32),
-            pltpu.SemaphoreType.DMA((4,)),
+            pltpu.SemaphoreType.DMA((5,)),
         ],
         compiler_params=pltpu.CompilerParams(vmem_limit_bytes=60 * MIB),
         name="share",
     )(targets, features, outside.reshape(1, rows), tiles)
-    arrived = exchange(share)
+    arrived = exchange(share, middle)
     together = half + 2 * fin + rows // 2
     total, links = pl.pallas_call(
         sum_kernel,
@@ -205,7 +226,7 @@
         node_kernel,
         out_shape=(
             pltpu.VMEM((rows, hidden), BF16),
-            pltpu.VMEM((peers, rows // 2 + max(slab, 16), hidden), BF16),
+            pltpu.VMEM((peers, rows // 4 + max(slab, 16), hidden), BF16),
             shape((rows, fin), F32),
         ),
         in_specs=[vmem] * 8,
@@ -219,27 +240,32 @@
         compiler_params=pltpu.CompilerParams(vmem_limit_bytes=(4 + peers // 8) * MIB),
         name="node",
     )(total, swap(total), links, outside, features, w_self, w_neigh, cotangent)
-    back = exchange(packed)
-    summed = jnp.sum(back[:, rows // 2 : rows // 2 + slab].astype(F32), axis=0).astype(BF16)
+    back = exchange(packed, middle)
+    half_back = back[:, : rows // 4]
+    pair = lax.ppermute(half_back, "dom", [(i, i ^ 1) for i in range(peers)])
     summed = pl.pallas_call(
         spread_kernel,
-        out_shape=pltpu.VMEM((peers, slab, hidden), BF16),
+        out_shape=pltpu.VMEM((owners, slab, hidden), BF16),
         in_specs=[vmem],
         out_specs=vmem,
-        compiler_params=pltpu.CompilerParams(vmem_limit_bytes=4 * MIB),
+        compiler_params=pltpu.CompilerParams(vmem_limit_bytes=(4 + peers // 16) * MIB),
         name="spread",
-    )(summed)
-    summed, back = lax.optimization_barrier((summed, back))
-    weight = exchange(summed)
+    )(back)
+    summed, half_back = lax.optimization_barrier((summed, half_back))
+    weight = exchange(summed, corner)
     term = pl.pallas_call(
         input_kernel,
         out_shape=shape((rows, fin), F32),
-        in_specs=[smem] + [vmem] * 3,
+        in_specs=[vmem] * 5,
         out_specs=vmem,
-        scratch_shapes=[pltpu.VMEM((peers, rows, fin), BF16)],
+        scratch_shapes=[
+            pltpu.SMEM((tile_count,), jnp.int32),
+            pltpu.VMEM((peers, rows, fin), BF16),
+            pltpu.SemaphoreType.DMA,
+        ],
         compiler_params=pltpu.CompilerParams(vmem_limit_bytes=(4 + peers // 8) * MIB),
         name="input",
-    )(targets, back, tiles, term)
+    )(targets, half_back, pair, tiles, term)
     block = shape((fin, hidden), F32)
     return pl.pallas_call(
         output_kernel,

time: 45.7 us -> 43.7 us (0.956)
  blocking collectives: 29.8 us -> 28.4 us
  local copies, waits for them, and re-layouts: 0.67 us -> 0.04 us
    ppermute x0 -> x1, starting transfers between devices: none -> 1.77 us  [on_device(): pair = lax.ppermute(half_back, 'dom', [(i, i ^ 1) for i in range(peers)])]
    all_to_all x1, starting transfers between devices: 6.48 us -> 5.1 us  [exchange(): lax.all_to_all(x, 'dom', split_axis=0, concat_axis=0, tiled=True, axis_in...]
    all_to_all x2, blocking collectives: 29.8 us -> 28.4 us  [exchange(): lax.all_to_all(x, 'dom', split_axis=0, concat_axis=0, tiled=True, axis_in...]
    ppermute x2, waiting for transfers between devices: 2.53 us -> 1.29 us  [swap(): return lax.ppermute(x, 'feat', [(0, 1), (1, 0)])]
    all_to_all x1, waiting for transfers between devices: 0.81 us -> 1.7 us  [exchange(): lax.all_to_all(x, 'dom', split_axis=0, concat_axis=0, tiled=True, axis_in...]
    unnamed x12 -> x10, local copies, waits for them, and re-layouts: 0.67 us -> 0.03 us
  transfers between devices with their start and end apart: 3 -> 4, of which waited for: 3 -> 2; matrix products, arithmetic and copies ran while one was open for 0% -> 0% of each run, Pallas kernels for 2% -> 3%
where the time goes in v3:
time: 43.7 us; the launch traced here: 43.3 us
  blocking collectives  28.4 us (65%)
  starting transfers between devices  7.01 us (16%)
  Pallas kernels  4.16 us (10%)
  waiting for transfers between devices  3 us (7%)
  between operations  0.73 us (2%)
    all_to_all x2, blocking collectives, exchange(): lax.all_to_all(x, 'dom', split_axis=0, concat_axis=0, tiled=True, axis_in...  28.4 us
    all_to_all x1, starting transfers between devices, exchange(): lax.all_to_all(x, 'dom', split_axis=0, concat_axis=0, tiled=True, axis_in...  5.1 us
    ppermute x1, starting transfers between devices, on_device(): pair = lax.ppermute(half_back, 'dom', [(i, i ^ 1) for i in range(peers)])  1.77 us
    all_to_all x1, waiting for transfers between devices, exchange(): lax.all_to_all(x, 'dom', split_axis=0, concat_axis=0, tiled=True, axis_in...  1.7 us
    pallas_call x1, Pallas kernels, on_device(): pl.pallas_call(share_kernel, out_shape=(pltpu.VMEM((peers, extended, rows...  1.47 us
    ppermute x2, waiting for transfers between devices, swap(): return lax.ppermute(x, 'feat', [(0, 1), (1, 0)])  1.29 us
  transfers between devices with their start and end apart: 4, of which 2 were waited for; matrix products, arithmetic and copies ran while one was open for 0% of the time, Pallas kernels for 3%

profile of v3, /device:TPU:0, one launch (start us, length us, event | category | flops | bytes accessed | tf_op | source)
XLA Modules:
  0.0 43.3 jit_solution(7169604182425223535)
XLA Ops:
  0.6 1.5 %share.1 = (bf16[16,72,128]{2,1,0:T(8,128)(2,1)S(1)}, s32[1,128]{1,0:T(1,128)S(1)}, s32[16]{0:T(128)S(1)}) custom-call(s32[16]{0:T(128)} %bitcast.4, bf16[128,128]{1,0:T(8,128)(2,1)} %features_ref.1, s32[1,128]{1,0:T(1,128)} %bitcast.5, bf16[16,128,128]{2,1,0:T(8,128)(2,1)} %tiles_ref.1), custom_call_target="tpu_custom_call" | custom-call | tf_op jit(solution)/shard_map/share/pallas_call | solution.py:195
  2.1 0.0 copy-start.2
  2.1 0.0 copy-start.3
  2.1 0.0 copy-start.4
  2.1 15.7 %all_to_all.15.arrived_ref = bf16[16,72,128]{2,1,0:T(8,128)(2,1)S(1)} all-to-all(bf16[16,72,128]{2,1,0:T(8,128)(2,1)S(1)} %get-tuple-element.14), channel_id=1, replica_groups={{22,6,30,14,18,2,26,10,20,4,28,12,16,0,24,8},{23,7,31,15,19,3,27,11,21,..., dimensions={0} | all-to-all | bytes 589824 | tf_op jit(solution)/shard_map/all_to_all | solution.py:188
  17.8 0.0 copy-done.2
  17.8 0.0 copy-done.3
  17.8 0.0 copy-done.4
  17.8 0.0 copy-start.1
  17.9 0.1 collective-permute-start
  18.0 1.3 %collective-permute-done.other_ref = bf16[384,128]{1,0:T(8,128)(2,1)S(1)} collective-permute-done((bf16[384,128]{1,0:T(8,128)(2,1)S(1)}, bf16[384,128]{1,0:T(8,128)(2,1)S(1)}, u32[]{:S(2)}, u32[]{:S(2)}) %collective-permute-start) | collective-permute-done | bytes 98336 | tf_op jit(solution)/shard_map/ppermute | solution.py:185
  19.2 0.0 copy-done.1
  19.2 0.4 %node.1 = (bf16[128,128]{1,0:T(8,128)(2,1)S(1)}, bf16[16,64,128]{2,1,0:T(8,128)(2,1)S(1)}, f32[128,128]{1,0:T(8,128)S(1)}) custom-call(bf16[384,128]{1,0:T(8,128)(2,1)S(1)} %get-tuple-element.15.total_ref, bf16[384,128]{1,0:T(8,128)(2,1)S(1)} %collective-permute-done.other_ref, f32[8,128]{1,0:T(8,128)S(1)} %get-tuple-element.16.links_ref, ...), custom_call_target="tpu_custom_call" | custom-call | tf_op jit(solution)/shard_map/node/pallas_call | solution.py:225
  19.7 0.0 copy-start
  19.7 12.8 %all_to_all.16.back_ref = bf16[16,64,128]{2,1,0:T(8,128)(2,1)S(1)} all-to-all(bf16[16,64,128]{2,1,0:T(8,128)(2,1)S(1)} %get-tuple-element.20), channel_id=1, replica_groups={{22,6,30,14,18,2,26,10,20,4,28,12,16,0,24,8},{23,7,31,15,19,3,27,11,21,..., dimensions={0} | all-to-all | bytes 524288 | tf_op jit(solution)/shard_map/all_to_all | solution.py:188
  32.5 1.8 %collective-permute-start.1 = (bf16[16,32,128]{2,1,0:T(8,128)(2,1)S(1)}, bf16[16,32,128]{2,1,0:T(8,128)(2,1)S(1)}, u32[]{:S(2)}, u32[]{:S(2)}) collective-permute-start(bf16[16,32,128]{2,1,0:T(8,128)(2,1)S(1)} %slice.4.back_ref), channel_id=1, source_target_pairs={{0,2},{2,0},{4,6},{6,4},{8,10},{10,8},{12,14},{14,12},{16,18},{18,... | collective-permute-start | bytes 393224 | tf_op jit(solution)/shard_map/ppermute | solution.py:245
  34.2 0.7 %spread.1 = bf16[8,32,128]{2,1,0:T(8,128)(2,1)} custom-call(bf16[16,64,128]{2,1,0:T(8,128)(2,1)S(1)} %all_to_all.16.back_ref), custom_call_target="tpu_custom_call" | custom-call | tf_op jit(solution)/shard_map/spread/pallas_call | solution.py:246
  34.9 5.1 %all-to-all-start.2 = ((bf16[8,32,128]{2,1,0:T(8,128)(2,1)}), bf16[8,32,128]{2,1,0:T(8,128)(2,1)S(1)}, u32[]{:S(2)}, u32[]{:S(2)}) async-start(bf16[8,32,128]{2,1,0:T(8,128)(2,1)} %spread.1), calls=%async_computation.2 | async-start | bytes 131072 | tf_op jit(solution)/shard_map/all_to_all | solution.py:188
  40.0 0.0 collective-permute-done.1.pair_ref
  40.0 0.0 copy-done
  40.0 0.9 %input.1.term_ref = f32[128,128]{1,0:T(8,128)S(1)} custom-call(s32[16]{0:T(128)S(1)} %get-tuple-element.19.targets_ref, bf16[16,32,128]{2,1,0:T(8,128)(2,1)S(1)} %slice.4.back_ref, bf16[16,32,128]{2,1,0:T(8,128)(2,1)S(1)} %collective-permute-done.1.pair_ref, bf16[16,128,128]{2,1,0:T(8,128)(2,1)S(1)} %copy-done, f32[128,128]{1,0:T(8,128)S(1)} %get-tuple-element.22.term_ref), custom_call_target="tpu_custom_call" | custom-call | tf_op jit(solution)/shard_map/input/pallas_call | solution.py:256
  40.9 0.1 collective-permute-start.2
  40.9 1.7 %all-to-all-done.2 = bf16[8,32,128]{2,1,0:T(8,128)(2,1)S(1)} async-done(((bf16[8,32,128]{2,1,0:T(8,128)(2,1)}), bf16[8,32,128]{2,1,0:T(8,128)(2,1)S(1)}, u32[]{:S(2)}, u32[]{:S(2)}) %all-to-all-start.2) | async-done | bytes 65568 | tf_op jit(solution)/shard_map/all_to_all | solution.py:188
  42.7 0.0 collective-permute-done.2.other_ref
  42.7 0.7 %outputs.1 = (bf16[128,128]{1,0:T(8,128)(2,1)}, bf16[128,128]{1,0:T(8,128)(2,1)}, f32[128,128]{1,0:T(8,128)}, f32[128,128]{1,0:T(8,128)}) custom-call(bf16[128,128]{1,0:T(8,128)(2,1)S(1)} %get-tuple-element.18.silu_ref, f32[128,128]{1,0:T(8,128)S(1)} %input.1.term_ref, f32[128,128]{1,0:T(8,128)S(1)} %collective-permute-done.2.other_ref, ...), custom_call_target="tpu_custom_call" | custom-call | tf_op jit(solution)/shard_map/outputs/pallas_call | solution.py:270
  (2 shorter events, 0.1 us)
Async XLA Ops:
  2.1 15.7 %copy-start.2 = (bf16[128,128]{1,0:T(8,128)(2,1)S(1)}, bf16[128,128]{1,0:T(8,128)(2,1)}, u32[]{:S(2)}) copy-start(bf16[128,128]{1,0:T(8,128)(2,1)} %w_self_ref.3) | copy-start | bytes 98308
  2.1 15.7 %copy-start.3 = (bf16[128,128]{1,0:T(8,128)(2,1)S(1)}, bf16[128,128]{1,0:T(8,128)(2,1)}, u32[]{:S(2)}) copy-start(bf16[128,128]{1,0:T(8,128)(2,1)} %w_neigh_ref.3) | copy-start | bytes 98308
  2.1 15.7 %copy-start.4 = (bf16[128,128]{1,0:T(8,128)(2,1)S(1)}, bf16[128,128]{1,0:T(8,128)(2,1)}, u32[]{:S(2)}) copy-start(bf16[128,128]{1,0:T(8,128)(2,1)} %cotangent_ref.3) | copy-start | bytes 98308
  17.8 1.4 %copy-start.1 = (bf16[128,128]{1,0:T(8,128)(2,1)S(1)}, bf16[128,128]{1,0:T(8,128)(2,1)}, u32[]{:S(2)}) copy-start(bf16[128,128]{1,0:T(8,128)(2,1)} %features_ref.1) | copy-start | bytes 98308
  17.9 1.4 %collective-permute-start = (bf16[384,128]{1,0:T(8,128)(2,1)S(1)}, bf16[384,128]{1,0:T(8,128)(2,1)S(1)}, u32[]{:S(2)}, u32[]{:S(2)}) collective-permute-start(bf16[384,128]{1,0:T(8,128)(2,1)S(1)} %get-tuple-element.15.total_ref), channel_id=1, source_target_pairs={{0,1},{1,0},{2,3},{3,2},{4,5},{5,4},{6,7},{7,6},{8,9},{9,8},{10,11... | collective-permute-start | bytes 294920 | tf_op jit(solution)/shard_map/ppermute | solution.py:185
  19.7 20.3 %copy-start = (bf16[16,128,128]{2,1,0:T(8,128)(2,1)S(1)}, bf16[16,128,128]{2,1,0:T(8,128)(2,1)}, u32[]{:S(2)}) copy-start(bf16[16,128,128]{2,1,0:T(8,128)(2,1)} %tiles_ref.1) | copy-start | bytes 1572868
  32.5 7.5 %collective-permute-start.1 = (bf16[16,32,128]{2,1,0:T(8,128)(2,1)S(1)}, bf16[16,32,128]{2,1,0:T(8,128)(2,1)S(1)}, u32[]{:S(2)}, u32[]{:S(2)}) collective-permute-start(bf16[16,32,128]{2,1,0:T(8,128)(2,1)S(1)} %slice.4.back_ref), channel_id=1, source_target_pairs={{0,2},{2,0},{4,6},{6,4},{8,10},{10,8},{12,14},{14,12},{16,18},{18,... | collective-permute-start | bytes 393224 | tf_op jit(solution)/shard_map/ppermute | solution.py:245
  34.9 7.8 %all-to-all-start.2 = ((bf16[8,32,128]{2,1,0:T(8,128)(2,1)}), bf16[8,32,128]{2,1,0:T(8,128)(2,1)S(1)}, u32[]{:S(2)}, u32[]{:S(2)}) async-start(bf16[8,32,128]{2,1,0:T(8,128)(2,1)} %spread.1), calls=%async_computation.2 | async-start | bytes 131072 | tf_op jit(solution)/shard_map/all_to_all | solution.py:188
  40.9 1.8 %collective-permute-start.2 = (f32[128,128]{1,0:T(8,128)S(1)}, f32[128,128]{1,0:T(8,128)S(1)}, u32[]{:S(2)}, u32[]{:S(2)}) collective-permute-start(f32[128,128]{1,0:T(8,128)S(1)} %input.1.term_ref), channel_id=1, source_target_pairs={{0,1},{1,0},{2,3},{3,2},{4,5},{5,4},{6,7},{7,6},{8,9},{9,8},{10,11... | collective-permute-start | bytes 196616 | tf_op jit(solution)/shard_map/ppermute | solution.py:185

commit v4 on v3

--- a/solution.py
+++ b/solution.py
@@ -9,6 +9,7 @@
 F32 = jnp.float32
 EXTRA = 8
 SHARERS = 2
+PAIR = 4
 MIB = 1 << 20
 
 NN = (((1,), (0,)), ((), ()))
@@ -45,19 +46,22 @@
     copies = [
         pltpu.make_async_copy(source, target, sems.at[i])
         for i, (source, target) in enumerate(
-            [(features_hbm, features_ref), (dest_hbm, dest_ref), (tiles_hbm, tiles_ref), (outside_hbm, outside_ref), (dest_hbm, targets_ref)]
+            [
+                (tiles_hbm, tiles_ref), (features_hbm, features_ref), (dest_hbm, dest_ref),
+                (outside_hbm, outside_ref), (dest_hbm, targets_ref),
+            ]
         )
     ]
     for copy in copies:
         copy.start()
     peers = sums_ref.shape[0]
     sums_ref[...] = jnp.zeros_like(sums_ref)
-    copies[0].wait()
+    copies[1].wait()
     turned_ref[...] = features_ref[...].T
     own, _ = halves(turned_ref.shape[0])
     left = jnp.concatenate([turned_ref[own, :], jnp.ones((EXTRA, turned_ref.shape[1]), BF16)], axis=0)
-    copies[1].wait()
     copies[2].wait()
+    copies[0].wait()
 
     def add(t):
         sums_ref[listed(dest_ref[t], peers)] += dot(left, tiles_ref[t], NN)
@@ -126,7 +130,8 @@
         weight = jnp.concatenate([weight, jnp.zeros((owners, packed - half - slab, hidden), F32)], axis=1)
     order = sorted(range(peers), key=lambda index: listed(index, peers))
     for k, index in enumerate(order):
-        packed_ref[k, :half] = back[(index & 1) * half : (index & 1) * half + half]
+        first = half if index & PAIR else 0
+        packed_ref[k, :half] = back[first : first + half]
         packed_ref[k, half:] = weight[listed(index % owners, owners, corner=True)].astype(BF16)
     term_ref[...] = dot(dpre, w_self_ref[...], NT)
 
@@ -138,7 +143,7 @@
     _, sibling = halves(tiles_ref.shape[2])
     quarter = half // 2
     first = lax.axis_index("feat") * half
-    odd = lax.axis_index("dom") & 1
+    odd = (lax.axis_index("dom") // PAIR) & 1
     padded_ref[:, pl.ds(pl.multiple_of(first + odd * quarter, quarter), quarter), :] = back_ref[...]
     padded_ref[:, pl.ds(pl.multiple_of(first + (1 - odd) * quarter, quarter), quarter), :] = pair_ref[...]
     padded_ref[:, sibling, :] = jnp.zeros((padded_ref.shape[0], half, padded_ref.shape[2]), BF16)
@@ -242,7 +247,7 @@
     )(total, swap(total), links, outside, features, w_self, w_neigh, cotangent)
     back = exchange(packed, middle)
     half_back = back[:, : rows // 4]
-    pair = lax.ppermute(half_back, "dom", [(i, i ^ 1) for i in range(peers)])
+    pair = lax.ppermute(half_back, "dom", [(i, i ^ PAIR) for i in range(peers)])
     summed = pl.pallas_call(
         spread_kernel,
         out_shape=pltpu.VMEM((owners, slab, hidden), BF16),

time: 43.7 us -> 43.3 us (level)
    ppermute x1, starting transfers between devices: 1.77 us -> 0.8 us  [on_device(): pair = lax.ppermute(half_back, 'dom', [(i, i ^ PAIR) for i in range(peers)])]
    all_to_all x1, starting transfers between devices: 5.1 us -> 5.72 us  [exchange(): lax.all_to_all(x, 'dom', split_axis=0, concat_axis=0, tiled=True, axis_in...]
  transfers between devices with their start and end apart: 4 -> 4, of which waited for: 2 -> 2; matrix products, arithmetic and copies ran while one was open for 0% -> 0% of each run, Pallas kernels for 3% -> 4%
where the time goes in v4:
time: 43.3 us; the launch traced here: 43 us
  blocking collectives  28.4 us (66%)
  starting transfers between devices  6.67 us (15%)
  Pallas kernels  4.14 us (10%)
  waiting for transfers between devices  2.99 us (7%)
  between operations  0.73 us (2%)
    all_to_all x2, blocking collectives, exchange(): lax.all_to_all(x, 'dom', split_axis=0, concat_axis=0, tiled=True, axis_in...  28.4 us
    all_to_all x1, starting transfers between devices, exchange(): lax.all_to_all(x, 'dom', split_axis=0, concat_axis=0, tiled=True, axis_in...  5.72 us
    all_to_all x1, waiting for transfers between devices, exchange(): lax.all_to_all(x, 'dom', split_axis=0, concat_axis=0, tiled=True, axis_in...  1.7 us
    pallas_call x1, Pallas kernels, on_device(): pl.pallas_call(share_kernel, out_shape=(pltpu.VMEM((peers, extended, rows...  1.45 us
    ppermute x2, waiting for transfers between devices, swap(): return lax.ppermute(x, 'feat', [(0, 1), (1, 0)])  1.29 us
  transfers between devices with their start and end apart: 4, of which 2 were waited for; matrix products, arithmetic and copies ran while one was open for 0% of the time, Pallas kernels for 4%

profile of v4, /device:TPU:0, one launch (start us, length us, event | category | flops | bytes accessed | tf_op | source)
XLA Modules:
  0.0 43.0 jit_solution(2206695762155075807)
XLA Ops:
  0.6 1.4 %share.1 = (bf16[16,72,128]{2,1,0:T(8,128)(2,1)S(1)}, s32[1,128]{1,0:T(1,128)S(1)}, s32[16]{0:T(128)S(1)}) custom-call(s32[16]{0:T(128)} %bitcast.4, bf16[128,128]{1,0:T(8,128)(2,1)} %features_ref.1, s32[1,128]{1,0:T(1,128)} %bitcast.5, bf16[16,128,128]{2,1,0:T(8,128)(2,1)} %tiles_ref.1), custom_call_target="tpu_custom_call" | custom-call | tf_op jit(solution)/shard_map/share/pallas_call | solution.py:200
  2.1 0.0 copy-start.2
  2.1 0.0 copy-start.3
  2.1 0.0 copy-start.4
  2.1 15.7 %all_to_all.15.arrived_ref = bf16[16,72,128]{2,1,0:T(8,128)(2,1)S(1)} all-to-all(bf16[16,72,128]{2,1,0:T(8,128)(2,1)S(1)} %get-tuple-element.14), channel_id=1, replica_groups={{22,6,30,14,18,2,26,10,20,4,28,12,16,0,24,8},{23,7,31,15,19,3,27,11,21,..., dimensions={0} | all-to-all | bytes 589824 | tf_op jit(solution)/shard_map/all_to_all | solution.py:193
  17.8 0.0 copy-done.2
  17.8 0.0 copy-done.3
  17.8 0.0 copy-done.4
  17.8 0.0 copy-start.1
  17.9 0.1 collective-permute-start
  17.9 1.3 %collective-permute-done.other_ref = bf16[384,128]{1,0:T(8,128)(2,1)S(1)} collective-permute-done((bf16[384,128]{1,0:T(8,128)(2,1)S(1)}, bf16[384,128]{1,0:T(8,128)(2,1)S(1)}, u32[]{:S(2)}, u32[]{:S(2)}) %collective-permute-start) | collective-permute-done | bytes 98336 | tf_op jit(solution)/shard_map/ppermute | solution.py:190
  19.2 0.0 copy-done.1
  19.2 0.4 %node.1 = (bf16[128,128]{1,0:T(8,128)(2,1)S(1)}, bf16[16,64,128]{2,1,0:T(8,128)(2,1)S(1)}, f32[128,128]{1,0:T(8,128)S(1)}) custom-call(bf16[384,128]{1,0:T(8,128)(2,1)S(1)} %get-tuple-element.15.total_ref, bf16[384,128]{1,0:T(8,128)(2,1)S(1)} %collective-permute-done.other_ref, f32[8,128]{1,0:T(8,128)S(1)} %get-tuple-element.16.links_ref, ...), custom_call_target="tpu_custom_call" | custom-call | tf_op jit(solution)/shard_map/node/pallas_call | solution.py:230
  19.7 0.0 copy-start
  19.7 12.8 %all_to_all.16.back_ref = bf16[16,64,128]{2,1,0:T(8,128)(2,1)S(1)} all-to-all(bf16[16,64,128]{2,1,0:T(8,128)(2,1)S(1)} %get-tuple-element.20), channel_id=1, replica_groups={{22,6,30,14,18,2,26,10,20,4,28,12,16,0,24,8},{23,7,31,15,19,3,27,11,21,..., dimensions={0} | all-to-all | bytes 524288 | tf_op jit(solution)/shard_map/all_to_all | solution.py:193
  32.4 0.8 %collective-permute-start.1 = (bf16[16,32,128]{2,1,0:T(8,128)(2,1)S(1)}, bf16[16,32,128]{2,1,0:T(8,128)(2,1)S(1)}, u32[]{:S(2)}, u32[]{:S(2)}) collective-permute-start(bf16[16,32,128]{2,1,0:T(8,128)(2,1)S(1)} %slice.4.back_ref), channel_id=1, source_target_pairs={{0,8},{2,10},{4,12},{6,14},{8,0},{10,2},{12,4},{14,6},{16,24},{18,... | collective-permute-start | bytes 393224 | tf_op jit(solution)/shard_map/ppermute | solution.py:250
  33.3 0.7 %spread.1 = bf16[8,32,128]{2,1,0:T(8,128)(2,1)} custom-call(bf16[16,64,128]{2,1,0:T(8,128)(2,1)S(1)} %all_to_all.16.back_ref), custom_call_target="tpu_custom_call" | custom-call | tf_op jit(solution)/shard_map/spread/pallas_call | solution.py:251
  33.9 5.7 %all-to-all-start.2 = ((bf16[8,32,128]{2,1,0:T(8,128)(2,1)}), bf16[8,32,128]{2,1,0:T(8,128)(2,1)S(1)}, u32[]{:S(2)}, u32[]{:S(2)}) async-start(bf16[8,32,128]{2,1,0:T(8,128)(2,1)} %spread.1), calls=%async_computation.2 | async-start | bytes 131072 | tf_op jit(solution)/shard_map/all_to_all | solution.py:193
  39.6 0.0 collective-permute-done.1.pair_ref
  39.6 0.0 copy-done
  39.6 0.9 %input.1.term_ref = f32[128,128]{1,0:T(8,128)S(1)} custom-call(s32[16]{0:T(128)S(1)} %get-tuple-element.19.targets_ref, bf16[16,32,128]{2,1,0:T(8,128)(2,1)S(1)} %slice.4.back_ref, bf16[16,32,128]{2,1,0:T(8,128)(2,1)S(1)} %collective-permute-done.1.pair_ref, bf16[16,128,128]{2,1,0:T(8,128)(2,1)S(1)} %copy-done, f32[128,128]{1,0:T(8,128)S(1)} %get-tuple-element.22.term_ref), custom_call_target="tpu_custom_call" | custom-call | tf_op jit(solution)/shard_map/input/pallas_call | solution.py:261
  40.5 0.1 collective-permute-start.2
  40.6 1.7 %all-to-all-done.2 = bf16[8,32,128]{2,1,0:T(8,128)(2,1)S(1)} async-done(((bf16[8,32,128]{2,1,0:T(8,128)(2,1)}), bf16[8,32,128]{2,1,0:T(8,128)(2,1)S(1)}, u32[]{:S(2)}, u32[]{:S(2)}) %all-to-all-start.2) | async-done | bytes 65568 | tf_op jit(solution)/shard_map/all_to_all | solution.py:193
  42.3 0.0 collective-permute-done.2.other_ref
  42.3 0.7 %outputs.1 = (bf16[128,128]{1,0:T(8,128)(2,1)}, bf16[128,128]{1,0:T(8,128)(2,1)}, f32[128,128]{1,0:T(8,128)}, f32[128,128]{1,0:T(8,128)}) custom-call(bf16[128,128]{1,0:T(8,128)(2,1)S(1)} %get-tuple-element.18.silu_ref, f32[128,128]{1,0:T(8,128)S(1)} %input.1.term_ref, f32[128,128]{1,0:T(8,128)S(1)} %collective-permute-done.2.other_ref, ...), custom_call_target="tpu_custom_call" | custom-call | tf_op jit(solution)/shard_map/outputs/pallas_call | solution.py:275
  (2 shorter events, 0.1 us)
Async XLA Ops:
  2.1 15.7 %copy-start.2 = (bf16[128,128]{1,0:T(8,128)(2,1)S(1)}, bf16[128,128]{1,0:T(8,128)(2,1)}, u32[]{:S(2)}) copy-start(bf16[128,128]{1,0:T(8,128)(2,1)} %w_self_ref.3) | copy-start | bytes 98308
  2.1 15.7 %copy-start.3 = (bf16[128,128]{1,0:T(8,128)(2,1)S(1)}, bf16[128,128]{1,0:T(8,128)(2,1)}, u32[]{:S(2)}) copy-start(bf16[128,128]{1,0:T(8,128)(2,1)} %w_neigh_ref.3) | copy-start | bytes 98308
  2.1 15.7 %copy-start.4 = (bf16[128,128]{1,0:T(8,128)(2,1)S(1)}, bf16[128,128]{1,0:T(8,128)(2,1)}, u32[]{:S(2)}) copy-start(bf16[128,128]{1,0:T(8,128)(2,1)} %cotangent_ref.3) | copy-start | bytes 98308
  17.8 1.4 %copy-start.1 = (bf16[128,128]{1,0:T(8,128)(2,1)S(1)}, bf16[128,128]{1,0:T(8,128)(2,1)}, u32[]{:S(2)}) copy-start(bf16[128,128]{1,0:T(8,128)(2,1)} %features_ref.1) | copy-start | bytes 98308
  17.9 1.4 %collective-permute-start = (bf16[384,128]{1,0:T(8,128)(2,1)S(1)}, bf16[384,128]{1,0:T(8,128)(2,1)S(1)}, u32[]{:S(2)}, u32[]{:S(2)}) collective-permute-start(bf16[384,128]{1,0:T(8,128)(2,1)S(1)} %get-tuple-element.15.total_ref), channel_id=1, source_target_pairs={{0,1},{1,0},{2,3},{3,2},{4,5},{5,4},{6,7},{7,6},{8,9},{9,8},{10,11... | collective-permute-start | bytes 294920 | tf_op jit(solution)/shard_map/ppermute | solution.py:190
  19.7 20.0 %copy-start = (bf16[16,128,128]{2,1,0:T(8,128)(2,1)S(1)}, bf16[16,128,128]{2,1,0:T(8,128)(2,1)}, u32[]{:S(2)}) copy-start(bf16[16,128,128]{2,1,0:T(8,128)(2,1)} %tiles_ref.1) | copy-start | bytes 1572868
  32.4 7.2 %collective-permute-start.1 = (bf16[16,32,128]{2,1,0:T(8,128)(2,1)S(1)}, bf16[16,32,128]{2,1,0:T(8,128)(2,1)S(1)}, u32[]{:S(2)}, u32[]{:S(2)}) collective-permute-start(bf16[16,32,128]{2,1,0:T(8,128)(2,1)S(1)} %slice.4.back_ref), channel_id=1, source_target_pairs={{0,8},{2,10},{4,12},{6,14},{8,0},{10,2},{12,4},{14,6},{16,24},{18,... | collective-permute-start | bytes 393224 | tf_op jit(solution)/shard_map/ppermute | solution.py:250
  33.9 8.4 %all-to-all-start.2 = ((bf16[8,32,128]{2,1,0:T(8,128)(2,1)}), bf16[8,32,128]{2,1,0:T(8,128)(2,1)S(1)}, u32[]{:S(2)}, u32[]{:S(2)}) async-start(bf16[8,32,128]{2,1,0:T(8,128)(2,1)} %spread.1), calls=%async_computation.2 | async-start | bytes 131072 | tf_op jit(solution)/shard_map/all_to_all | solution.py:193
  40.5 1.8 %collective-permute-start.2 = (f32[128,128]{1,0:T(8,128)S(1)}, f32[128,128]{1,0:T(8,128)S(1)}, u32[]{:S(2)}, u32[]{:S(2)}) collective-permute-start(f32[128,128]{1,0:T(8,128)S(1)} %input.1.term_ref), channel_id=1, source_target_pairs={{0,1},{1,0},{2,3},{3,2},{4,5},{5,4},{6,7},{7,6},{8,9},{9,8},{10,11... | collective-permute-start | bytes 196616 | tf_op jit(solution)/shard_map/ppermute | solution.py:190

commit v5 on v4

--- a/solution.py
+++ b/solution.py
@@ -86,7 +86,7 @@
 
 def node_kernel(
     total_ref, other_ref, links_ref, outside_ref, features_ref, w_self_ref, w_neigh_ref, cotangent_ref,
-    output_ref, packed_ref, term_ref, gathered_ref, nodes_ref, scale_ref, dagg_ref,
+    output_ref, packed_ref, dpre_ref, gathered_ref, nodes_ref, scale_ref, dagg_ref,
 ):
     fin, rows = gathered_ref.shape
     hidden = w_self_ref.shape[1]
@@ -133,10 +133,10 @@
         first = half if index & PAIR else 0
         packed_ref[k, :half] = back[first : first + half]
         packed_ref[k, half:] = weight[listed(index % owners, owners, corner=True)].astype(BF16)
-    term_ref[...] = dot(dpre, w_self_ref[...], NT)
-
-
-def input_kernel(targets_ref, back_ref, pair_ref, tiles_ref, term_ref, total_ref, dest_ref, padded_ref, sem):
+    dpre_ref[...] = dpre
+
+
+def input_kernel(targets_ref, back_ref, pair_ref, tiles_ref, dpre_ref, w_self_ref, total_ref, dest_ref, padded_ref, sem):
     copy = pltpu.make_async_copy(targets_ref, dest_ref, sem)
     copy.start()
     half = tiles_ref.shape[2] // 2
@@ -148,7 +148,7 @@
     padded_ref[:, pl.ds(pl.multiple_of(first + (1 - odd) * quarter, quarter), quarter), :] = pair_ref[...]
     padded_ref[:, sibling, :] = jnp.zeros((padded_ref.shape[0], half, padded_ref.shape[2]), BF16)
     peers = padded_ref.shape[0]
-    total = term_ref[...]
+    total = dot(dpre_ref[...], w_self_ref[...], NT)
     copy.wait()
     if tiles_ref.shape[0] <= 16:
         for t in range(tiles_ref.shape[0]):
@@ -227,12 +227,12 @@
         compiler_params=pltpu.CompilerParams(vmem_limit_bytes=(4 + peers // 8) * MIB),
         name="sum",
     )(arrived, w_self, w_neigh, cotangent)
-    output, packed, term = pl.pallas_call(
+    output, packed, dpre = pl.pallas_call(
         node_kernel,
         out_shape=(
             pltpu.VMEM((rows, hidden), BF16),
             pltpu.VMEM((peers, rows // 4 + max(slab, 16), hidden), BF16),
-            shape((rows, fin), F32),
+            pltpu.VMEM((rows, hidden), BF16),
         ),
         in_specs=[vmem] * 8,
         out_specs=(vmem,) * 3,
@@ -261,7 +261,7 @@
     term = pl.pallas_call(
         input_kernel,
         out_shape=shape((rows, fin), F32),
-        in_specs=[vmem] * 5,
+        in_specs=[vmem] * 6,
         out_specs=vmem,
         scratch_shapes=[
             pltpu.SMEM((tile_count,), jnp.int32),
@@ -270,7 +270,7 @@
         ],
         compiler_params=pltpu.CompilerParams(vmem_limit_bytes=(4 + peers // 8) * MIB),
         name="input",
-    )(targets, half_back, pair, tiles, term)
+    )(targets, half_back, pair, tiles, dpre, w_self)
     block = shape((fin, hidden), F32)
     return pl.pallas_call(
         output_kernel,

time: 43.3 us -> 43.3 us (level)
  no operation moved by 1% of the time
where the time goes in v5:
time: 43.3 us; the launch traced here: 43 us
  blocking collectives  28.4 us (66%)
  starting transfers between devices  6.67 us (15%)
  Pallas kernels  4.14 us (10%)
  waiting for transfers between devices  2.99 us (7%)
  between operations  0.73 us (2%)
    all_to_all x2, blocking collectives, exchange(): lax.all_to_all(x, 'dom', split_axis=0, concat_axis=0, tiled=True, axis_in...  28.4 us
    all_to_all x1, starting transfers between devices, exchange(): lax.all_to_all(x, 'dom', split_axis=0, concat_axis=0, tiled=True, axis_in...  5.72 us
    all_to_all x1, waiting for transfers between devices, exchange(): lax.all_to_all(x, 'dom', split_axis=0, concat_axis=0, tiled=True, axis_in...  1.7 us
    pallas_call x1, Pallas kernels, on_device(): pl.pallas_call(share_kernel, out_shape=(pltpu.VMEM((peers, extended, rows...  1.45 us
    ppermute x2, waiting for transfers between devices, swap(): return lax.ppermute(x, 'feat', [(0, 1), (1, 0)])  1.29 us
  transfers between devices with their start and end apart: 4, of which 2 were waited for; matrix products, arithmetic and copies ran while one was open for 0% of the time, Pallas kernels for 4%

profile of v5, /device:TPU:0, one launch (start us, length us, event | category | flops | bytes accessed | tf_op | source)
XLA Modules:
  0.0 43.0 jit_solution(12495125002441345164)
XLA Ops:
  0.6 1.5 %share.1 = (bf16[16,72,128]{2,1,0:T(8,128)(2,1)S(1)}, s32[1,128]{1,0:T(1,128)S(1)}, s32[16]{0:T(128)S(1)}) custom-call(s32[16]{0:T(128)} %bitcast.4, bf16[128,128]{1,0:T(8,128)(2,1)} %features_ref.1, s32[1,128]{1,0:T(1,128)} %bitcast.5, bf16[16,128,128]{2,1,0:T(8,128)(2,1)} %tiles_ref.1), custom_call_target="tpu_custom_call" | custom-call | tf_op jit(solution)/shard_map/share/pallas_call | solution.py:200
  2.1 0.0 copy-start.1
  2.1 0.0 copy-start.3
  2.1 0.0 copy-start.4
  2.1 15.7 %all_to_all.15.arrived_ref = bf16[16,72,128]{2,1,0:T(8,128)(2,1)S(1)} all-to-all(bf16[16,72,128]{2,1,0:T(8,128)(2,1)S(1)} %get-tuple-element.14), channel_id=1, replica_groups={{22,6,30,14,18,2,26,10,20,4,28,12,16,0,24,8},{23,7,31,15,19,3,27,11,21,..., dimensions={0} | all-to-all | bytes 589824 | tf_op jit(solution)/shard_map/all_to_all | solution.py:193
  17.8 0.0 copy-done.1
  17.8 0.0 copy-done.3
  17.8 0.0 copy-done.4
  17.8 0.0 copy-start.2
  17.9 0.1 collective-permute-start
  17.9 1.3 %collective-permute-done.other_ref = bf16[384,128]{1,0:T(8,128)(2,1)S(1)} collective-permute-done((bf16[384,128]{1,0:T(8,128)(2,1)S(1)}, bf16[384,128]{1,0:T(8,128)(2,1)S(1)}, u32[]{:S(2)}, u32[]{:S(2)}) %collective-permute-start) | collective-permute-done | bytes 98336 | tf_op jit(solution)/shard_map/ppermute | solution.py:190
  19.2 0.0 copy-done.2
  19.2 0.4 %node.1 = (bf16[128,128]{1,0:T(8,128)(2,1)S(1)}, bf16[16,64,128]{2,1,0:T(8,128)(2,1)S(1)}, bf16[128,128]{1,0:T(8,128)(2,1)S(1)}) custom-call(bf16[384,128]{1,0:T(8,128)(2,1)S(1)} %get-tuple-element.15.total_ref, bf16[384,128]{1,0:T(8,128)(2,1)S(1)} %collective-permute-done.other_ref, f32[8,128]{1,0:T(8,128)S(1)} %get-tuple-element.16.links_ref, ...), custom_call_target="tpu_custom_call" | custom-call | tf_op jit(solution)/shard_map/node/pallas_call | solution.py:230
  19.7 0.0 copy-start
  19.7 12.8 %all_to_all.16.back_ref = bf16[16,64,128]{2,1,0:T(8,128)(2,1)S(1)} all-to-all(bf16[16,64,128]{2,1,0:T(8,128)(2,1)S(1)} %get-tuple-element.20), channel_id=1, replica_groups={{22,6,30,14,18,2,26,10,20,4,28,12,16,0,24,8},{23,7,31,15,19,3,27,11,21,..., dimensions={0} | all-to-all | bytes 524288 | tf_op jit(solution)/shard_map/all_to_all | solution.py:193
  32.5 0.8 %collective-permute-start.1 = (bf16[16,32,128]{2,1,0:T(8,128)(2,1)S(1)}, bf16[16,32,128]{2,1,0:T(8,128)(2,1)S(1)}, u32[]{:S(2)}, u32[]{:S(2)}) collective-permute-start(bf16[16,32,128]{2,1,0:T(8,128)(2,1)S(1)} %slice.4.back_ref), channel_id=1, source_target_pairs={{0,8},{2,10},{4,12},{6,14},{8,0},{10,2},{12,4},{14,6},{16,24},{18,... | collective-permute-start | bytes 393224 | tf_op jit(solution)/shard_map/ppermute | solution.py:250
  33.3 0.7 %spread.1 = bf16[8,32,128]{2,1,0:T(8,128)(2,1)} custom-call(bf16[16,64,128]{2,1,0:T(8,128)(2,1)S(1)} %all_to_all.16.back_ref), custom_call_target="tpu_custom_call" | custom-call | tf_op jit(solution)/shard_map/spread/pallas_call | solution.py:251
  33.9 5.7 %all-to-all-start.2 = ((bf16[8,32,128]{2,1,0:T(8,128)(2,1)}), bf16[8,32,128]{2,1,0:T(8,128)(2,1)S(1)}, u32[]{:S(2)}, u32[]{:S(2)}) async-start(bf16[8,32,128]{2,1,0:T(8,128)(2,1)} %spread.1), calls=%async_computation.2 | async-start | bytes 131072 | tf_op jit(solution)/shard_map/all_to_all | solution.py:193
  39.6 0.0 collective-permute-done.1.pair_ref
  39.6 0.0 copy-done
  39.6 0.9 %input.1.term_ref = f32[128,128]{1,0:T(8,128)S(1)} custom-call(s32[16]{0:T(128)S(1)} %get-tuple-element.19.targets_ref, bf16[16,32,128]{2,1,0:T(8,128)(2,1)S(1)} %slice.4.back_ref, bf16[16,32,128]{2,1,0:T(8,128)(2,1)S(1)} %collective-permute-done.1.pair_ref, bf16[16,128,128]{2,1,0:T(8,128)(2,1)S(1)} %copy-done, ...), custom_call_target="tpu_custom_call" | custom-call | tf_op jit(solution)/shard_map/input/pallas_call | solution.py:261
  40.5 0.1 collective-permute-start.2
  40.6 1.7 %all-to-all-done.2 = bf16[8,32,128]{2,1,0:T(8,128)(2,1)S(1)} async-done(((bf16[8,32,128]{2,1,0:T(8,128)(2,1)}), bf16[8,32,128]{2,1,0:T(8,128)(2,1)S(1)}, u32[]{:S(2)}, u32[]{:S(2)}) %all-to-all-start.2) | async-done | bytes 65568 | tf_op jit(solution)/shard_map/all_to_all | solution.py:193
  42.3 0.0 collective-permute-done.2.other_ref
  42.3 0.7 %outputs.1 = (bf16[128,128]{1,0:T(8,128)(2,1)}, bf16[128,128]{1,0:T(8,128)(2,1)}, f32[128,128]{1,0:T(8,128)}, f32[128,128]{1,0:T(8,128)}) custom-call(bf16[128,128]{1,0:T(8,128)(2,1)S(1)} %get-tuple-element.18.silu_ref, f32[128,128]{1,0:T(8,128)S(1)} %input.1.term_ref, f32[128,128]{1,0:T(8,128)S(1)} %collective-permute-done.2.other_ref, ...), custom_call_target="tpu_custom_call" | custom-call | tf_op jit(solution)/shard_map/outputs/pallas_call | solution.py:275
  (2 shorter events, 0.1 us)
Async XLA Ops:
  2.1 15.7 %copy-start.1 = (bf16[128,128]{1,0:T(8,128)(2,1)S(1)}, bf16[128,128]{1,0:T(8,128)(2,1)}, u32[]{:S(2)}) copy-start(bf16[128,128]{1,0:T(8,128)(2,1)} %w_self_ref.5) | copy-start | bytes 98308
  2.1 15.7 %copy-start.3 = (bf16[128,128]{1,0:T(8,128)(2,1)S(1)}, bf16[128,128]{1,0:T(8,128)(2,1)}, u32[]{:S(2)}) copy-start(bf16[128,128]{1,0:T(8,128)(2,1)} %w_neigh_ref.3) | copy-start | bytes 98308
  2.1 15.7 %copy-start.4 = (bf16[128,128]{1,0:T(8,128)(2,1)S(1)}, bf16[128,128]{1,0:T(8,128)(2,1)}, u32[]{:S(2)}) copy-start(bf16[128,128]{1,0:T(8,128)(2,1)} %cotangent_ref.3) | copy-start | bytes 98308
  17.8 1.4 %copy-start.2 = (bf16[128,128]{1,0:T(8,128)(2,1)S(1)}, bf16[128,128]{1,0:T(8,128)(2,1)}, u32[]{:S(2)}) copy-start(bf16[128,128]{1,0:T(8,128)(2,1)} %features_ref.1) | copy-start | bytes 98308
  17.9 1.4 %collective-permute-start = (bf16[384,128]{1,0:T(8,128)(2,1)S(1)}, bf16[384,128]{1,0:T(8,128)(2,1)S(1)}, u32[]{:S(2)}, u32[]{:S(2)}) collective-permute-start(bf16[384,128]{1,0:T(8,128)(2,1)S(1)} %get-tuple-element.15.total_ref), channel_id=1, source_target_pairs={{0,1},{1,0},{2,3},{3,2},{4,5},{5,4},{6,7},{7,6},{8,9},{9,8},{10,11... | collective-permute-start | bytes 294920 | tf_op jit(solution)/shard_map/ppermute | solution.py:190
  19.7 20.0 %copy-start = (bf16[16,128,128]{2,1,0:T(8,128)(2,1)S(1)}, bf16[16,128,128]{2,1,0:T(8,128)(2,1)}, u32[]{:S(2)}) copy-start(bf16[16,128,128]{2,1,0:T(8,128)(2,1)} %tiles_ref.1) | copy-start | bytes 1572868
  32.5 7.2 %collective-permute-start.1 = (bf16[16,32,128]{2,1,0:T(8,128)(2,1)S(1)}, bf16[16,32,128]{2,1,0:T(8,128)(2,1)S(1)}, u32[]{:S(2)}, u32[]{:S(2)}) collective-permute-start(bf16[16,32,128]{2,1,0:T(8,128)(2,1)S(1)} %slice.4.back_ref), channel_id=1, source_target_pairs={{0,8},{2,10},{4,12},{6,14},{8,0},{10,2},{12,4},{14,6},{16,24},{18,... | collective-permute-start | bytes 393224 | tf_op jit(solution)/shard_map/ppermute | solution.py:250
  33.9 8.4 %all-to-all-start.2 = ((bf16[8,32,128]{2,1,0:T(8,128)(2,1)}), bf16[8,32,128]{2,1,0:T(8,128)(2,1)S(1)}, u32[]{:S(2)}, u32[]{:S(2)}) async-start(bf16[8,32,128]{2,1,0:T(8,128)(2,1)} %spread.1), calls=%async_computation.2 | async-start | bytes 131072 | tf_op jit(solution)/shard_map/all_to_all | solution.py:193
  40.5 1.8 %collective-permute-start.2 = (f32[128,128]{1,0:T(8,128)S(1)}, f32[128,128]{1,0:T(8,128)S(1)}, u32[]{:S(2)}, u32[]{:S(2)}) collective-permute-start(f32[128,128]{1,0:T(8,128)S(1)} %input.1.term_ref), channel_id=1, source_target_pairs={{0,1},{1,0},{2,3},{3,2},{4,5},{5,4},{6,7},{7,6},{8,9},{9,8},{10,11... | collective-permute-start | bytes 196616 | tf_op jit(solution)/shard_map/ppermute | solution.py:190

commit v6 on v5

--- a/solution.py
+++ b/solution.py
@@ -136,9 +136,13 @@
     dpre_ref[...] = dpre
 
 
-def input_kernel(targets_ref, back_ref, pair_ref, tiles_ref, dpre_ref, w_self_ref, total_ref, dest_ref, padded_ref, sem):
-    copy = pltpu.make_async_copy(targets_ref, dest_ref, sem)
+def input_kernel(
+    targets_ref, back_ref, pair_ref, tiles_ref, dpre_ref, w_self_ref, silu_ref, total_ref, output_hbm, dest_ref, padded_ref, sems,
+):
+    copy = pltpu.make_async_copy(targets_ref, dest_ref, sems.at[0])
+    write = pltpu.make_async_copy(silu_ref, output_hbm, sems.at[1])
     copy.start()
+    write.start()
     half = tiles_ref.shape[2] // 2
     _, sibling = halves(tiles_ref.shape[2])
     quarter = half // 2
@@ -158,6 +162,7 @@
             0, tiles_ref.shape[0], lambda t, sum: sum + dot(tiles_ref[t], padded_ref[listed(dest_ref[t], peers)], NN), total
         )
     total_ref[...] = total
+    write.wait()
 
 
 def spread_kernel(back_ref, parts_ref):
@@ -167,8 +172,7 @@
     parts_ref[...] = jnp.broadcast_to(part[None], parts_ref.shape)
 
 
-def output_kernel(silu_ref, term_ref, other_ref, weight_ref, output_ref, grad_input_ref, grad_self_ref, grad_neigh_ref):
-    output_ref[...] = silu_ref[...]
+def output_kernel(term_ref, other_ref, weight_ref, grad_input_ref, grad_self_ref, grad_neigh_ref):
     fin = grad_self_ref.shape[0]
     grad_input_ref[...] = (term_ref[...] + other_ref[...]).astype(BF16)
     grad_self_ref[...] = weight_ref[:fin].astype(F32)
@@ -258,28 +262,29 @@
     )(back)
     summed, half_back = lax.optimization_barrier((summed, half_back))
     weight = exchange(summed, corner)
-    term = pl.pallas_call(
+    term, output = pl.pallas_call(
         input_kernel,
-        out_shape=shape((rows, fin), F32),
-        in_specs=[vmem] * 6,
-        out_specs=vmem,
+        out_shape=(shape((rows, fin), F32), shape((rows, hidden), BF16)),
+        in_specs=[vmem] * 7,
+        out_specs=(vmem, hbm),
         scratch_shapes=[
             pltpu.SMEM((tile_count,), jnp.int32),
             pltpu.VMEM((peers, rows, fin), BF16),
-            pltpu.SemaphoreType.DMA,
+            pltpu.SemaphoreType.DMA((2,)),
         ],
         compiler_params=pltpu.CompilerParams(vmem_limit_bytes=(4 + peers // 8) * MIB),
         name="input",
-    )(targets, half_back, pair, tiles, dpre, w_self)
+    )(targets, half_back, pair, tiles, dpre, w_self, output)
     block = shape((fin, hidden), F32)
-    return pl.pallas_call(
+    gradients = pl.pallas_call(
         output_kernel,
-        out_shape=(shape((rows, hidden), BF16), shape((rows, fin), BF16), block, block),
-        in_specs=[vmem] * 4,
-        out_specs=(vmem,) * 4,
+        out_shape=(shape((rows, fin), BF16), block, block),
+        in_specs=[vmem] * 3,
+        out_specs=(vmem,) * 3,
         compiler_params=pltpu.CompilerParams(vmem_limit_bytes=4 * MIB),
         name="outputs",
-    )(output, term, swap(term), weight.reshape(2 * fin, hidden))
+    )(term, swap(term), weight.reshape(2 * fin, hidden))
+    return output, *gradients
 
 
 def solution(mesh):

time: 43.3 us -> 43.3 us (level)
  no operation moved by 1% of the time
where the time goes in v6:
time: 43.3 us; the launch traced here: 43 us
  blocking collectives  28.4 us (66%)
  starting transfers between devices  6.67 us (15%)
  Pallas kernels  4.14 us (10%)
  waiting for transfers between devices  2.98 us (7%)
  between operations  0.73 us (2%)
    all_to_all x2, blocking collectives, exchange(): lax.all_to_all(x, 'dom', split_axis=0, concat_axis=0, tiled=True, axis_in...  28.4 us
    all_to_all x1, starting transfers between devices, exchange(): lax.all_to_all(x, 'dom', split_axis=0, concat_axis=0, tiled=True, axis_in...  5.72 us
    all_to_all x1, waiting for transfers between devices, exchange(): lax.all_to_all(x, 'dom', split_axis=0, concat_axis=0, tiled=True, axis_in...  1.69 us
    pallas_call x1, Pallas kernels, on_device(): pl.pallas_call(share_kernel, out_shape=(pltpu.VMEM((peers, extended, rows...  1.45 us
    ppermute x2, waiting for transfers between devices, swap(): return lax.ppermute(x, 'feat', [(0, 1), (1, 0)])  1.29 us
    pallas_call x1, Pallas kernels, on_device(): pl.pallas_call(input_kernel, out_shape=(shape((rows, fin), F32), shape((r...  0.87 us
  transfers between devices with their start and end apart: 4, of which 2 were waited for; matrix products, arithmetic and copies ran while one was open for 0% of the time, Pallas kernels for 4%

profile of v6, /device:TPU:0, one launch (start us, length us, event | category | flops | bytes accessed | tf_op | source)
XLA Modules:
  0.0 43.0 jit_solution(5202426649304759637)
XLA Ops:
  0.6 1.4 %share.1 = (bf16[16,72,128]{2,1,0:T(8,128)(2,1)S(1)}, s32[1,128]{1,0:T(1,128)S(1)}, s32[16]{0:T(128)S(1)}) custom-call(s32[16]{0:T(128)} %bitcast.4, bf16[128,128]{1,0:T(8,128)(2,1)} %features_ref.1, s32[1,128]{1,0:T(1,128)} %bitcast.5, bf16[16,128,128]{2,1,0:T(8,128)(2,1)} %tiles_ref.1), custom_call_target="tpu_custom_call" | custom-call | tf_op jit(solution)/shard_map/share/pallas_call | solution.py:204
  2.1 0.0 copy-start.1
  2.1 0.0 copy-start.3
  2.1 0.0 copy-start.4
  2.1 15.7 %all_to_all.15.arrived_ref = bf16[16,72,128]{2,1,0:T(8,128)(2,1)S(1)} all-to-all(bf16[16,72,128]{2,1,0:T(8,128)(2,1)S(1)} %get-tuple-element.20), channel_id=1, replica_groups={{22,6,30,14,18,2,26,10,20,4,28,12,16,0,24,8},{23,7,31,15,19,3,27,11,21,..., dimensions={0} | all-to-all | bytes 589824 | tf_op jit(solution)/shard_map/all_to_all | solution.py:197
  17.8 0.0 copy-done.1
  17.8 0.0 copy-done.3
  17.8 0.0 copy-done.4
  17.8 0.0 copy-start.2
  17.9 0.1 collective-permute-start
  17.9 1.3 %collective-permute-done.other_ref = bf16[384,128]{1,0:T(8,128)(2,1)S(1)} collective-permute-done((bf16[384,128]{1,0:T(8,128)(2,1)S(1)}, bf16[384,128]{1,0:T(8,128)(2,1)S(1)}, u32[]{:S(2)}, u32[]{:S(2)}) %collective-permute-start) | collective-permute-done | bytes 98336 | tf_op jit(solution)/shard_map/ppermute | solution.py:194
  19.2 0.0 copy-done.2
  19.2 0.4 %node.1 = (bf16[128,128]{1,0:T(8,128)(2,1)S(1)}, bf16[16,64,128]{2,1,0:T(8,128)(2,1)S(1)}, bf16[128,128]{1,0:T(8,128)(2,1)S(1)}) custom-call(bf16[384,128]{1,0:T(8,128)(2,1)S(1)} %get-tuple-element.21.total_ref, bf16[384,128]{1,0:T(8,128)(2,1)S(1)} %collective-permute-done.other_ref, f32[8,128]{1,0:T(8,128)S(1)} %get-tuple-element.22.links_ref, ...), custom_call_target="tpu_custom_call" | custom-call | tf_op jit(solution)/shard_map/node/pallas_call | solution.py:234
  19.7 0.0 copy-start
  19.7 12.8 %all_to_all.16.back_ref = bf16[16,64,128]{2,1,0:T(8,128)(2,1)S(1)} all-to-all(bf16[16,64,128]{2,1,0:T(8,128)(2,1)S(1)} %get-tuple-element.24), channel_id=1, replica_groups={{22,6,30,14,18,2,26,10,20,4,28,12,16,0,24,8},{23,7,31,15,19,3,27,11,21,..., dimensions={0} | all-to-all | bytes 524288 | tf_op jit(solution)/shard_map/all_to_all | solution.py:197
  32.5 0.8 %collective-permute-start.1 = (bf16[16,32,128]{2,1,0:T(8,128)(2,1)S(1)}, bf16[16,32,128]{2,1,0:T(8,128)(2,1)S(1)}, u32[]{:S(2)}, u32[]{:S(2)}) collective-permute-start(bf16[16,32,128]{2,1,0:T(8,128)(2,1)S(1)} %slice.4.back_ref), channel_id=1, source_target_pairs={{0,8},{2,10},{4,12},{6,14},{8,0},{10,2},{12,4},{14,6},{16,24},{18,... | collective-permute-start | bytes 393224 | tf_op jit(solution)/shard_map/ppermute | solution.py:254
  33.3 0.7 %spread.1 = bf16[8,32,128]{2,1,0:T(8,128)(2,1)} custom-call(bf16[16,64,128]{2,1,0:T(8,128)(2,1)S(1)} %all_to_all.16.back_ref), custom_call_target="tpu_custom_call" | custom-call | tf_op jit(solution)/shard_map/spread/pallas_call | solution.py:255
  33.9 5.7 %all-to-all-start.2 = ((bf16[8,32,128]{2,1,0:T(8,128)(2,1)}), bf16[8,32,128]{2,1,0:T(8,128)(2,1)S(1)}, u32[]{:S(2)}, u32[]{:S(2)}) async-start(bf16[8,32,128]{2,1,0:T(8,128)(2,1)} %spread.1), calls=%async_computation.2 | async-start | bytes 131072 | tf_op jit(solution)/shard_map/all_to_all | solution.py:197
  39.6 0.0 collective-permute-done.1.pair_ref
  39.6 0.0 copy-done
  39.6 0.9 %input.1 = (f32[128,128]{1,0:T(8,128)S(1)}, bf16[128,128]{1,0:T(8,128)(2,1)}) custom-call(s32[16]{0:T(128)S(1)} %get-tuple-element.19.targets_ref, bf16[16,32,128]{2,1,0:T(8,128)(2,1)S(1)} %slice.4.back_ref, bf16[16,32,128]{2,1,0:T(8,128)(2,1)S(1)} %collective-permute-done.1.pair_ref, bf16[16,128,128]{2,1,0:T(8,128)(2,1)S(1)} %copy-done, ...), custom_call_target="tpu_custom_call" | custom-call | tf_op jit(solution)/shard_map/input/pallas_call | solution.py:265
  40.5 0.1 collective-permute-start.2
  40.6 1.7 %all-to-all-done.2 = bf16[8,32,128]{2,1,0:T(8,128)(2,1)S(1)} async-done(((bf16[8,32,128]{2,1,0:T(8,128)(2,1)}), bf16[8,32,128]{2,1,0:T(8,128)(2,1)S(1)}, u32[]{:S(2)}, u32[]{:S(2)}) %all-to-all-start.2) | async-done | bytes 65568 | tf_op jit(solution)/shard_map/all_to_all | solution.py:197
  42.3 0.0 collective-permute-done.2.other_ref
  42.3 0.7 %outputs.1 = (bf16[128,128]{1,0:T(8,128)(2,1)}, f32[128,128]{1,0:T(8,128)}, f32[128,128]{1,0:T(8,128)}) custom-call(f32[128,128]{1,0:T(8,128)S(1)} %get-tuple-element.29.term_ref, f32[128,128]{1,0:T(8,128)S(1)} %collective-permute-done.2.other_ref, bf16[256,128]{1,0:T(8,128)(2,1)S(1)} %bitcast.3), custom_call_target="tpu_custom_call" | custom-call | tf_op jit(solution)/shard_map/outputs/pallas_call | solution.py:279
  (2 shorter events, 0.1 us)
Async XLA Ops:
  2.1 15.7 %copy-start.1 = (bf16[128,128]{1,0:T(8,128)(2,1)S(1)}, bf16[128,128]{1,0:T(8,128)(2,1)}, u32[]{:S(2)}) copy-start(bf16[128,128]{1,0:T(8,128)(2,1)} %w_self_ref.5) | copy-start | bytes 98308
  2.1 15.7 %copy-start.3 = (bf16[128,128]{1,0:T(8,128)(2,1)S(1)}, bf16[128,128]{1,0:T(8,128)(2,1)}, u32[]{:S(2)}) copy-start(bf16[128,128]{1,0:T(8,128)(2,1)} %w_neigh_ref.3) | copy-start | bytes 98308
  2.1 15.7 %copy-start.4 = (bf16[128,128]{1,0:T(8,128)(2,1)S(1)}, bf16[128,128]{1,0:T(8,128)(2,1)}, u32[]{:S(2)}) copy-start(bf16[128,128]{1,0:T(8,128)(2,1)} %cotangent_ref.3) | copy-start | bytes 98308
  17.8 1.4 %copy-start.2 = (bf16[128,128]{1,0:T(8,128)(2,1)S(1)}, bf16[128,128]{1,0:T(8,128)(2,1)}, u32[]{:S(2)}) copy-start(bf16[128,128]{1,0:T(8,128)(2,1)} %features_ref.1) | copy-start | bytes 98308
  17.9 1.4 %collective-permute-start = (bf16[384,128]{1,0:T(8,128)(2,1)S(1)}, bf16[384,128]{1,0:T(8,128)(2,1)S(1)}, u32[]{:S(2)}, u32[]{:S(2)}) collective-permute-start(bf16[384,128]{1,0:T(8,128)(2,1)S(1)} %get-tuple-element.21.total_ref), channel_id=1, source_target_pairs={{0,1},{1,0},{2,3},{3,2},{4,5},{5,4},{6,7},{7,6},{8,9},{9,8},{10,11... | collective-permute-start | bytes 294920 | tf_op jit(solution)/shard_map/ppermute | solution.py:194
  19.7 20.0 %copy-start = (bf16[16,128,128]{2,1,0:T(8,128)(2,1)S(1)}, bf16[16,128,128]{2,1,0:T(8,128)(2,1)}, u32[]{:S(2)}) copy-start(bf16[16,128,128]{2,1,0:T(8,128)(2,1)} %tiles_ref.1) | copy-start | bytes 1572868
  32.5 7.2 %collective-permute-start.1 = (bf16[16,32,128]{2,1,0:T(8,128)(2,1)S(1)}, bf16[16,32,128]{2,1,0:T(8,128)(2,1)S(1)}, u32[]{:S(2)}, u32[]{:S(2)}) collective-permute-start(bf16[16,32,128]{2,1,0:T(8,128)(2,1)S(1)} %slice.4.back_ref), channel_id=1, source_target_pairs={{0,8},{2,10},{4,12},{6,14},{8,0},{10,2},{12,4},{14,6},{16,24},{18,... | collective-permute-start | bytes 393224 | tf_op jit(solution)/shard_map/ppermute | solution.py:254
  33.9 8.4 %all-to-all-start.2 = ((bf16[8,32,128]{2,1,0:T(8,128)(2,1)}), bf16[8,32,128]{2,1,0:T(8,128)(2,1)S(1)}, u32[]{:S(2)}, u32[]{:S(2)}) async-start(bf16[8,32,128]{2,1,0:T(8,128)(2,1)} %spread.1), calls=%async_computation.2 | async-start | bytes 131072 | tf_op jit(solution)/shard_map/all_to_all | solution.py:197
  40.5 1.8 %collective-permute-start.2 = (f32[128,128]{1,0:T(8,128)S(1)}, f32[128,128]{1,0:T(8,128)S(1)}, u32[]{:S(2)}, u32[]{:S(2)}) collective-permute-start(f32[128,128]{1,0:T(8,128)S(1)} %get-tuple-element.29.term_ref), channel_id=1, source_target_pairs={{0,1},{1,0},{2,3},{3,2},{4,5},{5,4},{6,7},{7,6},{8,9},{9,8},{10,11... | collective-permute-start | bytes 196616 | tf_op jit(solution)/shard_map/ppermute | solution.py:194

commit v7 on v5

--- a/solution.py
+++ b/solution.py
@@ -247,7 +247,6 @@
     )(total, swap(total), links, outside, features, w_self, w_neigh, cotangent)
     back = exchange(packed, middle)
     half_back = back[:, : rows // 4]
-    pair = lax.ppermute(half_back, "dom", [(i, i ^ PAIR) for i in range(peers)])
     summed = pl.pallas_call(
         spread_kernel,
         out_shape=pltpu.VMEM((owners, slab, hidden), BF16),
@@ -257,6 +256,7 @@
         name="spread",
     )(back)
     summed, half_back = lax.optimization_barrier((summed, half_back))
+    pair = lax.ppermute(half_back, "dom", [(i, i ^ PAIR) for i in range(peers)])
     weight = exchange(summed, corner)
     term = pl.pallas_call(
         input_kernel,

time: 43.3 us -> 43.3 us (level)
  transfers between devices with their start and end apart: 4 -> 4, of which waited for: 2 -> 2; matrix products, arithmetic and copies ran while one was open for 0% -> 0% of each run, Pallas kernels for 4% -> 2%
where the time goes in v7:
time: 43.3 us; the launch traced here: 43 us
  blocking collectives  28.4 us (66%)
  starting transfers between devices  6.67 us (15%)
  Pallas kernels  4.14 us (10%)
  waiting for transfers between devices  2.99 us (7%)
  between operations  0.73 us (2%)
    all_to_all x2, blocking collectives, exchange(): lax.all_to_all(x, 'dom', split_axis=0, concat_axis=0, tiled=True, axis_in...  28.4 us
    all_to_all x1, starting transfers between devices, exchange(): lax.all_to_all(x, 'dom', split_axis=0, concat_axis=0, tiled=True, axis_in...  5.72 us
    all_to_all x1, waiting for transfers between devices, exchange(): lax.all_to_all(x, 'dom', split_axis=0, concat_axis=0, tiled=True, axis_in...  1.7 us
    pallas_call x1, Pallas kernels, on_device(): pl.pallas_call(share_kernel, out_shape=(pltpu.VMEM((peers, extended, rows...  1.45 us
    ppermute x2, waiting for transfers between devices, swap(): return lax.ppermute(x, 'feat', [(0, 1), (1, 0)])  1.29 us
  transfers between devices with their start and end apart: 4, of which 2 were waited for; matrix products, arithmetic and copies ran while one was open for 0% of the time, Pallas kernels for 2%

profile of v7, /device:TPU:0, one launch (start us, length us, event | category | flops | bytes accessed | tf_op | source)
XLA Modules:
  0.0 43.0 jit_solution(5261445465587914765)
XLA Ops:
  0.6 1.4 %share.1 = (bf16[16,72,128]{2,1,0:T(8,128)(2,1)S(1)}, s32[1,128]{1,0:T(1,128)S(1)}, s32[16]{0:T(128)S(1)}) custom-call(s32[16]{0:T(128)} %bitcast.4, bf16[128,128]{1,0:T(8,128)(2,1)} %features_ref.1, s32[1,128]{1,0:T(1,128)} %bitcast.5, bf16[16,128,128]{2,1,0:T(8,128)(2,1)} %tiles_ref.1), custom_call_target="tpu_custom_call" | custom-call | tf_op jit(solution)/shard_map/share/pallas_call | solution.py:200
  2.1 0.0 copy-start.1
  2.1 0.0 copy-start.3
  2.1 0.0 copy-start.4
  2.1 15.7 %all_to_all.15.arrived_ref = bf16[16,72,128]{2,1,0:T(8,128)(2,1)S(1)} all-to-all(bf16[16,72,128]{2,1,0:T(8,128)(2,1)S(1)} %get-tuple-element.14), channel_id=1, replica_groups={{22,6,30,14,18,2,26,10,20,4,28,12,16,0,24,8},{23,7,31,15,19,3,27,11,21,..., dimensions={0} | all-to-all | bytes 589824 | tf_op jit(solution)/shard_map/all_to_all | solution.py:193
  17.8 0.0 copy-done.1
  17.8 0.0 copy-done.3
  17.8 0.0 copy-done.4
  17.8 0.0 copy-start.2
  17.8 0.1 collective-permute-start
  17.9 1.3 %collective-permute-done.other_ref = bf16[384,128]{1,0:T(8,128)(2,1)S(1)} collective-permute-done((bf16[384,128]{1,0:T(8,128)(2,1)S(1)}, bf16[384,128]{1,0:T(8,128)(2,1)S(1)}, u32[]{:S(2)}, u32[]{:S(2)}) %collective-permute-start) | collective-permute-done | bytes 98336 | tf_op jit(solution)/shard_map/ppermute | solution.py:190
  19.2 0.0 copy-done.2
  19.2 0.4 %node.1 = (bf16[128,128]{1,0:T(8,128)(2,1)S(1)}, bf16[16,64,128]{2,1,0:T(8,128)(2,1)S(1)}, bf16[128,128]{1,0:T(8,128)(2,1)S(1)}) custom-call(bf16[384,128]{1,0:T(8,128)(2,1)S(1)} %get-tuple-element.15.total_ref, bf16[384,128]{1,0:T(8,128)(2,1)S(1)} %collective-permute-done.other_ref, f32[8,128]{1,0:T(8,128)S(1)} %get-tuple-element.16.links_ref, ...), custom_call_target="tpu_custom_call" | custom-call | tf_op jit(solution)/shard_map/node/pallas_call | solution.py:230
  19.7 0.0 copy-start
  19.7 12.8 %all_to_all.16.back_ref = bf16[16,64,128]{2,1,0:T(8,128)(2,1)S(1)} all-to-all(bf16[16,64,128]{2,1,0:T(8,128)(2,1)S(1)} %get-tuple-element.20), channel_id=1, replica_groups={{22,6,30,14,18,2,26,10,20,4,28,12,16,0,24,8},{23,7,31,15,19,3,27,11,21,..., dimensions={0} | all-to-all | bytes 524288 | tf_op jit(solution)/shard_map/all_to_all | solution.py:193
  32.4 0.7 %spread.1 = bf16[8,32,128]{2,1,0:T(8,128)(2,1)} custom-call(bf16[16,64,128]{2,1,0:T(8,128)(2,1)S(1)} %all_to_all.16.back_ref), custom_call_target="tpu_custom_call" | custom-call | tf_op jit(solution)/shard_map/spread/pallas_call | solution.py:250
  33.1 0.8 %collective-permute-start.1 = (bf16[16,32,128]{2,1,0:T(8,128)(2,1)S(1)}, bf16[16,32,128]{2,1,0:T(8,128)(2,1)S(1)}, u32[]{:S(2)}, u32[]{:S(2)}) collective-permute-start(bf16[16,32,128]{2,1,0:T(8,128)(2,1)S(1)} %slice.4.back_ref), channel_id=1, source_target_pairs={{0,8},{2,10},{4,12},{6,14},{8,0},{10,2},{12,4},{14,6},{16,24},{18,... | collective-permute-start | bytes 393224 | tf_op jit(solution)/shard_map/ppermute | solution.py:259
  33.9 5.7 %all-to-all-start.2 = ((bf16[8,32,128]{2,1,0:T(8,128)(2,1)}), bf16[8,32,128]{2,1,0:T(8,128)(2,1)S(1)}, u32[]{:S(2)}, u32[]{:S(2)}) async-start(bf16[8,32,128]{2,1,0:T(8,128)(2,1)} %spread.1), calls=%async_computation.2 | async-start | bytes 131072 | tf_op jit(solution)/shard_map/all_to_all | solution.py:193
  39.6 0.0 collective-permute-done.1.pair_ref
  39.6 0.0 copy-done
  39.6 0.9 %input.1.term_ref = f32[128,128]{1,0:T(8,128)S(1)} custom-call(s32[16]{0:T(128)S(1)} %get-tuple-element.19.targets_ref, bf16[16,32,128]{2,1,0:T(8,128)(2,1)S(1)} %slice.4.back_ref, bf16[16,32,128]{2,1,0:T(8,128)(2,1)S(1)} %collective-permute-done.1.pair_ref, bf16[16,128,128]{2,1,0:T(8,128)(2,1)S(1)} %copy-done, ...), custom_call_target="tpu_custom_call" | custom-call | tf_op jit(solution)/shard_map/input/pallas_call | solution.py:261
  40.5 0.1 collective-permute-start.2
  40.6 1.7 %all-to-all-done.2 = bf16[8,32,128]{2,1,0:T(8,128)(2,1)S(1)} async-done(((bf16[8,32,128]{2,1,0:T(8,128)(2,1)}), bf16[8,32,128]{2,1,0:T(8,128)(2,1)S(1)}, u32[]{:S(2)}, u32[]{:S(2)}) %all-to-all-start.2) | async-done | bytes 65568 | tf_op jit(solution)/shard_map/all_to_all | solution.py:193
  42.3 0.0 collective-permute-done.2.other_ref
  42.3 0.7 %outputs.1 = (bf16[128,128]{1,0:T(8,128)(2,1)}, bf16[128,128]{1,0:T(8,128)(2,1)}, f32[128,128]{1,0:T(8,128)}, f32[128,128]{1,0:T(8,128)}) custom-call(bf16[128,128]{1,0:T(8,128)(2,1)S(1)} %get-tuple-element.18.silu_ref, f32[128,128]{1,0:T(8,128)S(1)} %input.1.term_ref, f32[128,128]{1,0:T(8,128)S(1)} %collective-permute-done.2.other_ref, ...), custom_call_target="tpu_custom_call" | custom-call | tf_op jit(solution)/shard_map/outputs/pallas_call | solution.py:275
  (2 shorter events, 0.1 us)
Async XLA Ops:
  2.1 15.7 %copy-start.1 = (bf16[128,128]{1,0:T(8,128)(2,1)S(1)}, bf16[128,128]{1,0:T(8,128)(2,1)}, u32[]{:S(2)}) copy-start(bf16[128,128]{1,0:T(8,128)(2,1)} %w_self_ref.5) | copy-start | bytes 98308
  2.1 15.7 %copy-start.3 = (bf16[128,128]{1,0:T(8,128)(2,1)S(1)}, bf16[128,128]{1,0:T(8,128)(2,1)}, u32[]{:S(2)}) copy-start(bf16[128,128]{1,0:T(8,128)(2,1)} %w_neigh_ref.3) | copy-start | bytes 98308
  2.1 15.7 %copy-start.4 = (bf16[128,128]{1,0:T(8,128)(2,1)S(1)}, bf16[128,128]{1,0:T(8,128)(2,1)}, u32[]{:S(2)}) copy-start(bf16[128,128]{1,0:T(8,128)(2,1)} %cotangent_ref.3) | copy-start | bytes 98308
  17.8 1.4 %copy-start.2 = (bf16[128,128]{1,0:T(8,128)(2,1)S(1)}, bf16[128,128]{1,0:T(8,128)(2,1)}, u32[]{:S(2)}) copy-start(bf16[128,128]{1,0:T(8,128)(2,1)} %features_ref.1) | copy-start | bytes 98308
  17.8 1.4 %collective-permute-start = (bf16[384,128]{1,0:T(8,128)(2,1)S(1)}, bf16[384,128]{1,0:T(8,128)(2,1)S(1)}, u32[]{:S(2)}, u32[]{:S(2)}) collective-permute-start(bf16[384,128]{1,0:T(8,128)(2,1)S(1)} %get-tuple-element.15.total_ref), channel_id=1, source_target_pairs={{0,1},{1,0},{2,3},{3,2},{4,5},{5,4},{6,7},{7,6},{8,9},{9,8},{10,11... | collective-permute-start | bytes 294920 | tf_op jit(solution)/shard_map/ppermute | solution.py:190
  19.7 20.0 %copy-start = (bf16[16,128,128]{2,1,0:T(8,128)(2,1)S(1)}, bf16[16,128,128]{2,1,0:T(8,128)(2,1)}, u32[]{:S(2)}) copy-start(bf16[16,128,128]{2,1,0:T(8,128)(2,1)} %tiles_ref.1) | copy-start | bytes 1572868
  33.1 6.5 %collective-permute-start.1 = (bf16[16,32,128]{2,1,0:T(8,128)(2,1)S(1)}, bf16[16,32,128]{2,1,0:T(8,128)(2,1)S(1)}, u32[]{:S(2)}, u32[]{:S(2)}) collective-permute-start(bf16[16,32,128]{2,1,0:T(8,128)(2,1)S(1)} %slice.4.back_ref), channel_id=1, source_target_pairs={{0,8},{2,10},{4,12},{6,14},{8,0},{10,2},{12,4},{14,6},{16,24},{18,... | collective-permute-start | bytes 393224 | tf_op jit(solution)/shard_map/ppermute | solution.py:259
  33.9 8.4 %all-to-all-start.2 = ((bf16[8,32,128]{2,1,0:T(8,128)(2,1)}), bf16[8,32,128]{2,1,0:T(8,128)(2,1)S(1)}, u32[]{:S(2)}, u32[]{:S(2)}) async-start(bf16[8,32,128]{2,1,0:T(8,128)(2,1)} %spread.1), calls=%async_computation.2 | async-start | bytes 131072 | tf_op jit(solution)/shard_map/all_to_all | solution.py:193
  40.5 1.8 %collective-permute-start.2 = (f32[128,128]{1,0:T(8,128)S(1)}, f32[128,128]{1,0:T(8,128)S(1)}, u32[]{:S(2)}, u32[]{:S(2)}) collective-permute-start(f32[128,128]{1,0:T(8,128)S(1)} %input.1.term_ref), channel_id=1, source_target_pairs={{0,1},{1,0},{2,3},{3,2},{4,5},{5,4},{6,7},{7,6},{8,9},{9,8},{10,11... | collective-permute-start | bytes 196616 | tf_op jit(solution)/shard_map/ppermute | solution.py:190

commit v8 on v5

--- a/solution.py
+++ b/solution.py
@@ -28,9 +28,9 @@
         pl.loop(0, count)(body)
 
 
-def listed(index, peers, corner=False):
+def listed(index, peers, corner=False, near=False):
     bits = peers.bit_length() - 1
-    index = index ^ (peers - 1 if corner else peers - peers // 4 - 1)
+    index = index ^ (peers - 1 if corner else peers // 2 - 1 if near else peers - peers // 4 - 1)
     return sum(((index >> bit) & 1) << (bits - 1 - bit) for bit in range(bits))
 
 
@@ -128,7 +128,7 @@
     weight = weight.reshape(owners, slab, hidden)
     if packed - half > slab:
         weight = jnp.concatenate([weight, jnp.zeros((owners, packed - half - slab, hidden), F32)], axis=1)
-    order = sorted(range(peers), key=lambda index: listed(index, peers))
+    order = sorted(range(peers), key=lambda index: listed(index, peers, near=True))
     for k, index in enumerate(order):
         first = half if index & PAIR else 0
         packed_ref[k, :half] = back[first : first + half]
@@ -152,10 +152,10 @@
     copy.wait()
     if tiles_ref.shape[0] <= 16:
         for t in range(tiles_ref.shape[0]):
-            total = total + dot(tiles_ref[t], padded_ref[listed(dest_ref[t], peers)], NN)
+            total = total + dot(tiles_ref[t], padded_ref[listed(dest_ref[t], peers, near=True)], NN)
     else:
         total = lax.fori_loop(
-            0, tiles_ref.shape[0], lambda t, sum: sum + dot(tiles_ref[t], padded_ref[listed(dest_ref[t], peers)], NN), total
+            0, tiles_ref.shape[0], lambda t, sum: sum + dot(tiles_ref[t], padded_ref[listed(dest_ref[t], peers, near=True)], NN), total
         )
     total_ref[...] = total
 
@@ -193,6 +193,7 @@
         return lax.all_to_all(x, "dom", split_axis=0, concat_axis=0, tiled=True, axis_index_groups=groups)
 
     middle = [sorted(range(peers), key=lambda index: listed(index, peers))]
+    near = [sorted(range(peers), key=lambda index: listed(index, peers, near=True))]
     owners = peers // SHARERS
     corner = sorted(range(owners), key=lambda index: listed(index, owners, corner=True))
     corner = [[first + index for index in corner] for first in range(0, peers, owners)]
@@ -245,7 +246,7 @@
         compiler_params=pltpu.CompilerParams(vmem_limit_bytes=(4 + peers // 8) * MIB),
         name="node",
     )(total, swap(total), links, outside, features, w_self, w_neigh, cotangent)
-    back = exchange(packed, middle)
+    back = exchange(packed, near)
     half_back = back[:, : rows // 4]
     pair = lax.ppermute(half_back, "dom", [(i, i ^ PAIR) for i in range(peers)])
     summed = pl.pallas_call(

time: 43.3 us -> 44.1 us (1.018)
  blocking collectives: 28.4 us -> 29.7 us
  starting transfers between devices: 6.67 us -> 6.07 us
    all_to_all x2, blocking collectives: 28.4 us -> 29.7 us  [exchange(): lax.all_to_all(x, 'dom', split_axis=0, concat_axis=0, tiled=True, axis_in...]
  transfers between devices with their start and end apart: 4 -> 4, of which waited for: 2 -> 2; matrix products, arithmetic and copies ran while one was open for 0% -> 0% of each run, Pallas kernels for 4% -> 3%
where the time goes in v8:
time: 44.1 us; the launch traced here: 43.7 us
  blocking collectives  29.7 us (67%)
  starting transfers between devices  6.07 us (14%)
  Pallas kernels  4.14 us (9%)
  waiting for transfers between devices  2.99 us (7%)
  between operations  0.73 us (2%)
    all_to_all x2, blocking collectives, exchange(): lax.all_to_all(x, 'dom', split_axis=0, concat_axis=0, tiled=True, axis_in...  29.7 us
    all_to_all x1, starting transfers between devices, exchange(): lax.all_to_all(x, 'dom', split_axis=0, concat_axis=0, tiled=True, axis_in...  5.48 us
    all_to_all x1, waiting for transfers between devices, exchange(): lax.all_to_all(x, 'dom', split_axis=0, concat_axis=0, tiled=True, axis_in...  1.7 us
    pallas_call x1, Pallas kernels, on_device(): pl.pallas_call(share_kernel, out_shape=(pltpu.VMEM((peers, extended, rows...  1.45 us
    ppermute x2, waiting for transfers between devices, swap(): return lax.ppermute(x, 'feat', [(0, 1), (1, 0)])  1.29 us
  transfers between devices with their start and end apart: 4, of which 2 were waited for; matrix products, arithmetic and copies ran while one was open for 0% of the time, Pallas kernels for 3%

profile of v8, /device:TPU:0, one launch (start us, length us, event | category | flops | bytes accessed | tf_op | source)
XLA Modules:
  0.0 43.7 jit_solution(4199010594750122954)
XLA Ops:
  0.6 1.4 %share.1 = (bf16[16,72,128]{2,1,0:T(8,128)(2,1)S(1)}, s32[1,128]{1,0:T(1,128)S(1)}, s32[16]{0:T(128)S(1)}) custom-call(s32[16]{0:T(128)} %bitcast.4, bf16[128,128]{1,0:T(8,128)(2,1)} %features_ref.1, s32[1,128]{1,0:T(1,128)} %bitcast.5, bf16[16,128,128]{2,1,0:T(8,128)(2,1)} %tiles_ref.1), custom_call_target="tpu_custom_call" | custom-call | tf_op jit(solution)/shard_map/share/pallas_call | solution.py:201
  2.1 0.0 copy-start.1
  2.1 0.0 copy-start.3
  2.1 0.0 copy-start.4
  2.1 15.7 %all_to_all.15.arrived_ref = bf16[16,72,128]{2,1,0:T(8,128)(2,1)S(1)} all-to-all(bf16[16,72,128]{2,1,0:T(8,128)(2,1)S(1)} %get-tuple-element.14), channel_id=1, replica_groups={{22,6,30,14,18,2,26,10,20,4,28,12,16,0,24,8},{23,7,31,15,19,3,27,11,21,..., dimensions={0} | all-to-all | bytes 589824 | tf_op jit(solution)/shard_map/all_to_all | solution.py:193
  17.8 0.0 copy-done.1
  17.8 0.0 copy-done.3
  17.8 0.0 copy-done.4
  17.8 0.0 copy-start.2
  17.8 0.1 collective-permute-start
  17.9 1.3 %collective-permute-done.other_ref = bf16[384,128]{1,0:T(8,128)(2,1)S(1)} collective-permute-done((bf16[384,128]{1,0:T(8,128)(2,1)S(1)}, bf16[384,128]{1,0:T(8,128)(2,1)S(1)}, u32[]{:S(2)}, u32[]{:S(2)}) %collective-permute-start) | collective-permute-done | bytes 98336 | tf_op jit(solution)/shard_map/ppermute | solution.py:190
  19.2 0.0 copy-done.2
  19.2 0.4 %node.1 = (bf16[128,128]{1,0:T(8,128)(2,1)S(1)}, bf16[16,64,128]{2,1,0:T(8,128)(2,1)S(1)}, bf16[128,128]{1,0:T(8,128)(2,1)S(1)}) custom-call(bf16[384,128]{1,0:T(8,128)(2,1)S(1)} %get-tuple-element.15.total_ref, bf16[384,128]{1,0:T(8,128)(2,1)S(1)} %collective-permute-done.other_ref, f32[8,128]{1,0:T(8,128)S(1)} %get-tuple-element.16.links_ref, ...), custom_call_target="tpu_custom_call" | custom-call | tf_op jit(solution)/shard_map/node/pallas_call | solution.py:231
  19.7 0.0 copy-start
  19.7 14.1 %all_to_all.16.back_ref = bf16[16,64,128]{2,1,0:T(8,128)(2,1)S(1)} all-to-all(bf16[16,64,128]{2,1,0:T(8,128)(2,1)S(1)} %get-tuple-element.20), channel_id=1, replica_groups={{14,30,6,22,10,26,2,18,12,28,4,20,8,24,0,16},{15,31,7,23,11,27,3,19,13,..., dimensions={0} | all-to-all | bytes 524288 | tf_op jit(solution)/shard_map/all_to_all | solution.py:193
  33.8 0.5 %collective-permute-start.1 = (bf16[16,32,128]{2,1,0:T(8,128)(2,1)S(1)}, bf16[16,32,128]{2,1,0:T(8,128)(2,1)S(1)}, u32[]{:S(2)}, u32[]{:S(2)}) collective-permute-start(bf16[16,32,128]{2,1,0:T(8,128)(2,1)S(1)} %slice.4.back_ref), channel_id=1, source_target_pairs={{0,8},{2,10},{4,12},{6,14},{8,0},{10,2},{12,4},{14,6},{16,24},{18,... | collective-permute-start | bytes 393224 | tf_op jit(solution)/shard_map/ppermute | solution.py:251
  34.2 0.7 %spread.1 = bf16[8,32,128]{2,1,0:T(8,128)(2,1)} custom-call(bf16[16,64,128]{2,1,0:T(8,128)(2,1)S(1)} %all_to_all.16.back_ref), custom_call_target="tpu_custom_call" | custom-call | tf_op jit(solution)/shard_map/spread/pallas_call | solution.py:252
  34.9 5.5 %all-to-all-start.2 = ((bf16[8,32,128]{2,1,0:T(8,128)(2,1)}), bf16[8,32,128]{2,1,0:T(8,128)(2,1)S(1)}, u32[]{:S(2)}, u32[]{:S(2)}) async-start(bf16[8,32,128]{2,1,0:T(8,128)(2,1)} %spread.1), calls=%async_computation.2 | async-start | bytes 131072 | tf_op jit(solution)/shard_map/all_to_all | solution.py:193
  40.4 0.0 collective-permute-done.1.pair_ref
  40.4 0.0 copy-done
  40.4 0.9 %input.1.term_ref = f32[128,128]{1,0:T(8,128)S(1)} custom-call(s32[16]{0:T(128)S(1)} %get-tuple-element.19.targets_ref, bf16[16,32,128]{2,1,0:T(8,128)(2,1)S(1)} %slice.4.back_ref, bf16[16,32,128]{2,1,0:T(8,128)(2,1)S(1)} %collective-permute-done.1.pair_ref, bf16[16,128,128]{2,1,0:T(8,128)(2,1)S(1)} %copy-done, ...), custom_call_target="tpu_custom_call" | custom-call | tf_op jit(solution)/shard_map/input/pallas_call | solution.py:262
  41.2 0.1 collective-permute-start.2
  41.3 1.7 %all-to-all-done.2 = bf16[8,32,128]{2,1,0:T(8,128)(2,1)S(1)} async-done(((bf16[8,32,128]{2,1,0:T(8,128)(2,1)}), bf16[8,32,128]{2,1,0:T(8,128)(2,1)S(1)}, u32[]{:S(2)}, u32[]{:S(2)}) %all-to-all-start.2) | async-done | bytes 65568 | tf_op jit(solution)/shard_map/all_to_all | solution.py:193
  43.0 0.0 collective-permute-done.2.other_ref
  43.0 0.7 %outputs.1 = (bf16[128,128]{1,0:T(8,128)(2,1)}, bf16[128,128]{1,0:T(8,128)(2,1)}, f32[128,128]{1,0:T(8,128)}, f32[128,128]{1,0:T(8,128)}) custom-call(bf16[128,128]{1,0:T(8,128)(2,1)S(1)} %get-tuple-element.18.silu_ref, f32[128,128]{1,0:T(8,128)S(1)} %input.1.term_ref, f32[128,128]{1,0:T(8,128)S(1)} %collective-permute-done.2.other_ref, ...), custom_call_target="tpu_custom_call" | custom-call | tf_op jit(solution)/shard_map/outputs/pallas_call | solution.py:276
  (2 shorter events, 0.1 us)
Async XLA Ops:
  2.1 15.7 %copy-start.1 = (bf16[128,128]{1,0:T(8,128)(2,1)S(1)}, bf16[128,128]{1,0:T(8,128)(2,1)}, u32[]{:S(2)}) copy-start(bf16[128,128]{1,0:T(8,128)(2,1)} %w_self_ref.5) | copy-start | bytes 98308
  2.1 15.7 %copy-start.3 = (bf16[128,128]{1,0:T(8,128)(2,1)S(1)}, bf16[128,128]{1,0:T(8,128)(2,1)}, u32[]{:S(2)}) copy-start(bf16[128,128]{1,0:T(8,128)(2,1)} %w_neigh_ref.3) | copy-start | bytes 98308
  2.1 15.7 %copy-start.4 = (bf16[128,128]{1,0:T(8,128)(2,1)S(1)}, bf16[128,128]{1,0:T(8,128)(2,1)}, u32[]{:S(2)}) copy-start(bf16[128,128]{1,0:T(8,128)(2,1)} %cotangent_ref.3) | copy-start | bytes 98308
  17.8 1.4 %copy-start.2 = (bf16[128,128]{1,0:T(8,128)(2,1)S(1)}, bf16[128,128]{1,0:T(8,128)(2,1)}, u32[]{:S(2)}) copy-start(bf16[128,128]{1,0:T(8,128)(2,1)} %features_ref.1) | copy-start | bytes 98308
  17.8 1.4 %collective-permute-start = (bf16[384,128]{1,0:T(8,128)(2,1)S(1)}, bf16[384,128]{1,0:T(8,128)(2,1)S(1)}, u32[]{:S(2)}, u32[]{:S(2)}) collective-permute-start(bf16[384,128]{1,0:T(8,128)(2,1)S(1)} %get-tuple-element.15.total_ref), channel_id=1, source_target_pairs={{0,1},{1,0},{2,3},{3,2},{4,5},{5,4},{6,7},{7,6},{8,9},{9,8},{10,11... | collective-permute-start | bytes 294920 | tf_op jit(solution)/shard_map/ppermute | solution.py:190
  19.7 20.7 %copy-start = (bf16[16,128,128]{2,1,0:T(8,128)(2,1)S(1)}, bf16[16,128,128]{2,1,0:T(8,128)(2,1)}, u32[]{:S(2)}) copy-start(bf16[16,128,128]{2,1,0:T(8,128)(2,1)} %tiles_ref.1) | copy-start | bytes 1572868
  33.8 6.6 %collective-permute-start.1 = (bf16[16,32,128]{2,1,0:T(8,128)(2,1)S(1)}, bf16[16,32,128]{2,1,0:T(8,128)(2,1)S(1)}, u32[]{:S(2)}, u32[]{:S(2)}) collective-permute-start(bf16[16,32,128]{2,1,0:T(8,128)(2,1)S(1)} %slice.4.back_ref), channel_id=1, source_target_pairs={{0,8},{2,10},{4,12},{6,14},{8,0},{10,2},{12,4},{14,6},{16,24},{18,... | collective-permute-start | bytes 393224 | tf_op jit(solution)/shard_map/ppermute | solution.py:251
  34.9 8.1 %all-to-all-start.2 = ((bf16[8,32,128]{2,1,0:T(8,128)(2,1)}), bf16[8,32,128]{2,1,0:T(8,128)(2,1)S(1)}, u32[]{:S(2)}, u32[]{:S(2)}) async-start(bf16[8,32,128]{2,1,0:T(8,128)(2,1)} %spread.1), calls=%async_computation.2 | async-start | bytes 131072 | tf_op jit(solution)/shard_map/all_to_all | solution.py:193
  41.2 1.8 %collective-permute-start.2 = (f32[128,128]{1,0:T(8,128)S(1)}, f32[128,128]{1,0:T(8,128)S(1)}, u32[]{:S(2)}, u32[]{:S(2)}) collective-permute-start(f32[128,128]{1,0:T(8,128)S(1)} %input.1.term_ref), channel_id=1, source_target_pairs={{0,1},{1,0},{2,3},{3,2},{4,5},{5,4},{6,7},{7,6},{8,9},{9,8},{10,11... | collective-permute-start | bytes 196616 | tf_op jit(solution)/shard_map/ppermute | solution.py:190
